TPU v7x, 128 devices: a whole 4x4x4 slice. The times are simulated.
128 devices in a mesh: lon: 16 (over y, z_hi, core), lat: 8 (over x, z_lo).
Axes of the slice: x: 4, y: 4, z: 4 (z_hi: 2, z_lo: 2; z = z_hi * 2 + z_lo), core: 2. Of those that a mesh axis runs over, the one named last changes fastest.
Arguments:
- grid_state: bfloat16 [64, 1024, 256], P('lat', 'lon'), may hold values from -6 to 6
- encodings: bfloat16 [12288, 2, 256], P(('lon', 'lat')), may hold values from -6 to 6
- routes: int32 [12288, 2], replicated, may hold values from 0 to 127, all different within a row; in each aligned block of 96 rows (0 to 95, 96 to 191, ...) at most 2 rows name the same one
- w_query: bfloat16 [256, 256], replicated, may hold values from -0.375 to 0.375
- w_key: bfloat16 [256, 256], replicated, may hold values from -0.375 to 0.375
- w_value: bfloat16 [256, 256], replicated, may hold values from -0.375 to 0.375
- w_out: bfloat16 [256, 256], replicated, may hold values from -0.375 to 0.375
- kernels: bfloat16 [2, 7, 7, 256], replicated, may hold values from -0.875 to 0.875
- w_expand: bfloat16 [2, 256, 1024], replicated, may hold values from -0.375 to 0.375
- w_reduce: bfloat16 [2, 1024, 256], replicated, may hold values from -0.1875 to 0.1875
- cotangent: bfloat16 [64, 1024, 256], P('lat', 'lon'), may hold values from -6 to 6
Outputs:
- analysis: bfloat16 [64, 1024, 256], P('lat', 'lon')
- grad_encodings: float32 [12288, 2, 256], P(('lon', 'lat'))
- grad_attention: float32 [4, 256, 256], replicated
- grad_kernels: float32 [2, 7, 7, 256], replicated
- grad_expand: float32 [2, 256, 1024], replicated
- grad_reduce: float32 [2, 1024, 256], replicated
Inputs may be any that keep to these rules, and one draw needn't show every extreme that they name: `routes`: each block names 2 different tiles; among the 96 blocks of one device at most 2 name the same tile, and exactly 2 in some device; every tile is named by some block.
All inputs are finite; a program needn't handle non-finite values.
Results may differ from a plain program's by a relative error of at most 0.022.
Values may be sent and summed in bfloat16 or wider, within the bound.
A program may use at most 128 MiB of HBM per device.

v0:
```python
import functools
import math

import jax
import jax.numpy as jnp
from jax import lax
from jax.experimental import pallas as pl
from jax.experimental.pallas import tpu as pltpu
from jax.sharding import PartitionSpec as P

MESH = pl.DeviceIdType.MESH
F32 = jnp.float32
BF16 = jnp.bfloat16

HEADS = 8
DEPTH = 32
CH = 256
WIDE = 1024
ROWS = 8
COLS = 64
CELLS = ROWS * COLS
NLON = 16
NLAT = 8
NYZ = 8
DEVICES = NLON * NLAT
BLOCKS_DEV = 96
SLOTS = 512
EPSILON = 1e-06
SCALE = 1.0 / math.sqrt(DEPTH)
GELU_0 = math.sqrt(2.0 / math.pi)
GELU_1 = GELU_0 * 0.044715
PAD_ROWS = ROWS + 6
PAD_COLS = 80
BIG = 2048
KROWS = 128


def mm(a, b):
    return jnp.dot(a, b, preferred_element_type=F32)


def mm_nt(a, b):
    return lax.dot_general(a, b, (((1,), (1,)), ((), ())), preferred_element_type=F32)


def mm_tn(a, b):
    return lax.dot_general(a, b, (((0,), (0,)), ((), ())), preferred_element_type=F32)


def loop(low, high, body):
    def step(index, carry):
        body(index)
        return carry

    lax.fori_loop(low, high, step, 0)


def aligned(value, by):
    return pl.multiple_of(value, by)


class Exchange:
    def __init__(self, place, source, half, level_1, part, level_2, total, sems, rows):
        self.lon, self.lat, self.core, self.yz = place
        self.source, self.half, self.level_1 = source, half, level_1
        self.part, self.level_2, self.total = part, level_2, total
        self.sems = sems
        self.r1, self.r2, self.r3 = rows // 2, rows // 16, rows // 128

    def copy(self, src, dst, index, lon, lat):
        return pltpu.make_async_remote_copy(
            src_ref=src,
            dst_ref=dst,
            send_sem=self.sems.at[0, index],
            recv_sem=self.sems.at[1, index],
            device_id=(lon, lat),
            device_id_type=MESH,
        )

    def pair(self):
        return self.lon + 1 - 2 * self.core

    def lat_peer(self, k):
        return lax.rem(self.lat + k, NLAT)

    def lat_from(self, k):
        return lax.rem(self.lat + NLAT - k, NLAT)

    def yz_peer(self, k):
        return lax.rem(self.yz + k, NYZ)

    def yz_from(self, k):
        return lax.rem(self.yz + NYZ - k, NYZ)

    def copy_0(self):
        other = aligned((1 - self.core) * self.r1, self.r1)
        return self.copy(
            self.source.at[pl.ds(other, self.r1)], self.half.at[...], 0, self.pair(), self.lat
        )

    def start_0(self):
        self.copy_0().start()

    def copy_1(self, k):
        peer = self.lat_peer(k)
        return self.copy(
            self.half.at[pl.ds(aligned(peer * self.r2, self.r2), self.r2)],
            self.level_1.at[k],
            k,
            self.lon,
            peer,
        )

    def start_1(self):
        self.copy_0().wait()
        mine = aligned(self.core * self.r1, self.r1)
        step = self.r1 // 4

        def add(i):
            at = aligned(i * step, step)
            self.half[pl.ds(at, step)] = (
                self.half[pl.ds(at, step)].astype(F32)
                + self.source[pl.ds(aligned(mine + at, step), step)].astype(F32)
            ).astype(BF16)

        loop(0, 4, add)
        loop(1, NLAT, lambda k: self.copy_1(k).start())

    def copy_2(self, k):
        peer = self.yz_peer(k)
        return self.copy(
            self.part.at[pl.ds(aligned(peer * self.r3, self.r3), self.r3)],
            self.level_2.at[k],
            8 + k,
            peer * 2 + self.core,
            self.lat,
        )

    def start_2(self):
        loop(1, NLAT, lambda k: self.copy_1(k).wait())
        total = self.half[pl.ds(aligned(self.lat * self.r2, self.r2), self.r2)].astype(F32)
        for k in range(1, NLAT):
            total = total + self.level_1[k].astype(F32)
        self.part[...] = total.astype(BF16)
        loop(1, NYZ, lambda k: self.copy_2(k).start())

    def offset(self, core, lat, yz):
        return core * self.r1 + lat * self.r2 + yz * self.r3

    def copy_3(self, k):
        rows = pl.ds(aligned(self.offset(self.core, self.lat, self.yz), self.r3), self.r3)
        return self.copy(
            self.total.at[rows],
            self.total.at[rows],
            16 + k,
            self.yz_peer(k) * 2 + self.core,
            self.lat,
        )

    def start_3(self):
        loop(1, NYZ, lambda k: self.copy_2(k).wait())
        total = self.part[pl.ds(aligned(self.yz * self.r3, self.r3), self.r3)].astype(F32)
        for k in range(1, NYZ):
            total = total + self.level_2[k].astype(F32)
        rows = pl.ds(aligned(self.offset(self.core, self.lat, self.yz), self.r3), self.r3)
        self.total[rows] = total.astype(BF16)
        loop(1, NYZ, lambda k: self.copy_3(k).start())

    def copy_4(self, k):
        rows = pl.ds(aligned(self.offset(self.core, self.lat, 0), self.r2), self.r2)
        return self.copy(
            self.total.at[rows], self.total.at[rows], 24 + k, self.lon, self.lat_peer(k)
        )

    def start_4(self):
        def settle(k):
            self.copy_3(k).wait_send()
            rows = pl.ds(
                aligned(self.offset(self.core, self.lat, self.yz_from(k)), self.r3), self.r3
            )
            self.copy(
                self.total.at[rows], self.total.at[rows], 16 + k, self.lon, self.lat
            ).wait_recv()

        loop(1, NYZ, settle)
        loop(1, NLAT, lambda k: self.copy_4(k).start())

    def copy_5(self):
        rows = pl.ds(aligned(self.core * self.r1, self.r1), self.r1)
        return self.copy(self.total.at[rows], self.total.at[rows], 8, self.pair(), self.lat)

    def start_5(self):
        def settle(k):
            self.copy_4(k).wait_send()
            rows = pl.ds(aligned(self.offset(self.core, self.lat_from(k), 0), self.r2), self.r2)
            self.copy(
                self.total.at[rows], self.total.at[rows], 24 + k, self.lon, self.lat
            ).wait_recv()

        loop(1, NLAT, settle)
        self.copy_5().start()

    def finish(self):
        self.copy_5().wait_send()
        rows = pl.ds(aligned((1 - self.core) * self.r1, self.r1), self.r1)
        self.copy(
            self.total.at[rows], self.total.at[rows], 8, self.lon, self.lat
        ).wait_recv()


class SmallExchange:
    def __init__(self, place, source, level_1, part, level_2, total, sems):
        self.lon, self.lat, self.core, self.yz = place
        self.source, self.level_1, self.part = source, level_1, part
        self.level_2, self.total, self.sems = level_2, total, sems

    def copy(self, src, dst, index, lon, lat):
        return pltpu.make_async_remote_copy(
            src_ref=src,
            dst_ref=dst,
            send_sem=self.sems.at[0, index],
            recv_sem=self.sems.at[1, index],
            device_id=(lon, lat),
            device_id_type=MESH,
        )

    def copy_0(self, k):
        peer = lax.rem(self.lat + k, NLAT)
        return self.copy(
            self.source.at[pl.ds(aligned(peer * 16, 16), 16)], self.level_1.at[k], k, self.lon, peer
        )

    def start_0(self):
        loop(1, NLAT, lambda k: self.copy_0(k).start())

    def copy_1(self, k):
        peer = lax.rem(self.lon + k, NLON)
        return self.copy(self.part.at[...], self.level_2.at[k], 8 + k, peer, self.lat)

    def start_1(self):
        loop(1, NLAT, lambda k: self.copy_0(k).wait())
        total = self.source[pl.ds(aligned(self.lat * 16, 16), 16)].astype(F32)
        for k in range(1, NLAT):
            total = total + self.level_1[k].astype(F32)
        self.part[...] = total.astype(BF16)
        loop(1, NLON, lambda k: self.copy_1(k).start())

    def copy_2(self, k):
        rows = pl.ds(aligned(self.lat * 16, 16), 16)
        peer = lax.rem(self.lat + k, NLAT)
        return self.copy(self.total.at[rows], self.total.at[rows], 24 + k, self.lon, peer)

    def start_2(self):
        loop(1, NLON, lambda k: self.copy_1(k).wait())
        self.level_2[0] = self.part[...]
        total = jnp.zeros((16, CH), F32)
        for index in range(NLON):
            slot = lax.rem(self.lon - index + NLON, NLON)
            total = total + self.level_2[slot].astype(F32)
        self.total[pl.ds(aligned(self.lat * 16, 16), 16)] = total.astype(BF16)
        loop(1, NLAT, lambda k: self.copy_2(k).start())

    def finish(self):
        def settle(k):
            self.copy_2(k).wait_send()
            rows = pl.ds(aligned(lax.rem(self.lat + NLAT - k, NLAT) * 16, 16), 16)
            self.copy(
                self.total.at[rows], self.total.at[rows], 24 + k, self.lon, self.lat
            ).wait_recv()

        loop(1, NLAT, settle)


class Halo:
    def __init__(self, place, tile, rows, cols, corners, sems):
        self.lon, self.lat = place[0], place[1]
        self.tile, self.rows, self.cols, self.corners, self.sems = tile, rows, cols, corners, sems

    def copies(self):
        east, west = lax.rem(self.lon + 1, NLON), lax.rem(self.lon + NLON - 1, NLON)
        south, north = lax.rem(self.lat + 1, NLAT), lax.rem(self.lat + NLAT - 1, NLAT)
        top, bottom, whole = pl.ds(0, 3), pl.ds(ROWS - 3, 3), pl.ds(0, ROWS)
        left, right, wide = pl.ds(0, 16), pl.ds(COLS - 16, 16), pl.ds(0, COLS)
        plan = [
            (top, wide, self.rows.at[1], self.lon, north),
            (bottom, wide, self.rows.at[0], self.lon, south),
            (whole, left, self.cols.at[1], west, self.lat),
            (whole, right, self.cols.at[0], east, self.lat),
            (top, left, self.corners.at[3], west, north),
            (top, right, self.corners.at[2], east, north),
            (bottom, left, self.corners.at[1], west, south),
            (bottom, right, self.corners.at[0], east, south),
        ]
        return [
            pltpu.make_async_remote_copy(
                src_ref=self.tile.at[r, c],
                dst_ref=dst,
                send_sem=self.sems.at[0, index],
                recv_sem=self.sems.at[1, index],
                device_id=(lon, lat),
                device_id_type=MESH,
            )
            for index, (r, c, dst, lon, lat) in enumerate(plan)
        ]

    def start(self):
        for copy in self.copies():
            copy.start()

    def fill_inner(self, padded):
        for row in range(ROWS):
            cells = self.tile[row].astype(F32)
            for half in range(2):
                padded[half, 3 + row, 8 : 8 + COLS, :] = cells[:, half * 128 : half * 128 + 128]

    def fill_edges(self, padded):
        for copy in self.copies():
            copy.wait()
        has_north = jnp.where(self.lat > 0, 1.0, 0.0).astype(F32)
        has_south = jnp.where(self.lat < NLAT - 1, 1.0, 0.0).astype(F32)
        for half in range(2):
            lanes = slice(half * 128, half * 128 + 128)
            for row in range(ROWS):
                padded[half, 3 + row, 0:8, :] = self.cols[0, row, 8:16, lanes].astype(F32)
                padded[half, 3 + row, 72:80, :] = self.cols[1, row, 0:8, lanes].astype(F32)
            for row in range(3):
                for side, there, start in ((0, has_north, 0), (1, has_south, 3 + ROWS)):
                    padded[half, start + row, 8 : 8 + COLS, :] = (
                        self.rows[side, row, :, lanes].astype(F32) * there
                    )
                    padded[half, start + row, 0:8, :] = (
                        self.corners[2 * side, row, 8:16, lanes].astype(F32) * there
                    )
                    padded[half, start + row, 72:80, :] = (
                        self.corners[2 * side + 1, row, 0:8, lanes].astype(F32) * there
                    )


def correlate(padded, taps, block, flipped, store):
    def one_half(half):
        for chunk in range(4):
            sums = [None] * ROWS
            for b in range(7):
                rows = [
                    padded[half, row, chunk * 16 + b + 5 : chunk * 16 + b + 21, :]
                    for row in range(PAD_ROWS)
                ]
                for a in range(7):
                    tap_id = (6 - a) * 7 + (6 - b) if flipped else a * 7 + b
                    tap = taps[half, tap_id, block : block + 1, :]
                    for row in range(ROWS):
                        term = rows[row + a] * tap
                        sums[row] = term if sums[row] is None else sums[row] + term
            store(half, chunk, sums)

    loop(0, 2, one_half)


def kernel_grads(padded, inner, results, block):
    def one_half(half):
        for b in range(7):
            sums = [None] * 7
            for chunk in range(8):
                rows = [
                    padded[half, row, chunk * 8 + b + 5 : chunk * 8 + b + 13, :]
                    for row in range(PAD_ROWS)
                ]
                grads = [
                    inner[half, row, chunk * 8 : chunk * 8 + 8, :] for row in range(ROWS)
                ]
                for a in range(7):
                    for row in range(ROWS):
                        term = rows[row + a] * grads[row]
                        sums[a] = term if sums[a] is None else sums[a] + term
            for a in range(7):
                results[half, pl.ds(block * 56 + a * 7 + b, 1), :] = jnp.sum(
                    sums[a], axis=0, keepdims=True
                )

    loop(0, 2, one_half)


def iota(shape, dim):
    return lax.broadcasted_iota(jnp.int32, shape, dim)


def one_hot(condition):
    return jnp.where(condition, 1.0, 0.0).astype(BF16)


def normalise(values):
    centred = values - jnp.mean(values, axis=-1, keepdims=True)
    spread = jnp.mean(centred * centred, axis=-1, keepdims=True)
    scale = lax.rsqrt(spread + EPSILON)
    return centred * scale, scale


def kernel(
    grid_ref,
    enc_ref,
    routes_ref,
    wq_ref,
    wk_ref,
    wv_ref,
    wo_ref,
    kernels_ref,
    we_ref,
    wr_ref,
    cot_ref,
    analysis_ref,
    grad_enc_ref,
    out_attention,
    out_kernels,
    out_1,
    out_0,
    chosen_ref,
    send_a,
    recv_a,
    send_b,
    recv_b,
    back_b,
    got_b,
    back_a,
    got_a,
    live_ref,
    normed_ref,
    q_ref,
    qt_ref,
    k_ref,
    kt_ref,
    v_ref,
    vt_ref,
    probs_ref,
    ctx_t_ref,
    st_ref,
    gl_ref,
    pad_ref,
    pad_back,
    inner_ref,
    taps_ref,
    kgrad_ref,
    xhat_ref,
    rstd_ref,
    nrm_ref,
    wide_ref,
    dgelu_ref,
    gpre_ref,
    grad_ref,
    low_ref,
    gctx_ref,
    gt_ref,
    dq_t_ref,
    dk_ref,
    dv_ref,
    halo_rows,
    halo_cols,
    halo_corners,
    x_attention,
    x_kernels,
    x_1,
    x_0,
    half_att,
    half_1,
    half_0,
    l1_att,
    l1_1,
    l1_0,
    part_att,
    part_1,
    part_0,
    l2_att,
    l2_1,
    l2_0,
    l1_k,
    part_k,
    l2_k,
    a2a_sems,
    halo_sems,
    sems_att,
    sems_1,
    sems_0,
    sems_k,
):
    lon, lat = lax.axis_index("lon"), lax.axis_index("lat")
    core, yz = lax.rem(lon, 2), lon // 2
    place = (lon, lat, core, yz)
    me = lon * NLAT + lat

    barrier = pltpu.get_barrier_semaphore()

    def greet(to_lon, to_lat):
        pl.semaphore_signal(barrier, inc=1, device_id=(to_lon, to_lat), device_id_type=MESH)

    loop(1, NLAT, lambda k: greet(lon, lax.rem(lat + k, NLAT)))
    loop(1, NLON, lambda k: greet(lax.rem(lon + k, NLON), lat))
    for dx in (1, NLON - 1):
        for dy in (1, NLAT - 1):
            greet(lax.rem(lon + dx, NLON), lax.rem(lat + dy, NLAT))

    row_id = iota((DEVICES, BLOCKS_DEV), 0)
    tile_id = lax.rem(row_id, NLON) * NLAT + row_id // NLON
    hits = (routes_ref[0, pl.ds(me, 1), :] == tile_id) | (
        routes_ref[1, pl.ds(me, 1), :] == tile_id
    )
    before = one_hot(iota((BLOCKS_DEV, BLOCKS_DEV), 0) < iota((BLOCKS_DEV, BLOCKS_DEV), 1))
    hot = one_hot(hits)
    earlier = mm(hot, before)
    for c in range(2):
        chosen = jnp.where(jnp.abs(earlier - c) < 0.5, hot.astype(F32), 0.0).astype(BF16)
        chosen_ref[c] = chosen
        send_a[:, c * 512 : c * 512 + 512] = mm(chosen, enc_ref[...]).astype(BF16)

    pl.semaphore_wait(barrier, NLAT - 1 + NLON - 1 + 4)

    def a2a(src, dst, index, to_lon, to_lat):
        return pltpu.make_async_remote_copy(
            src_ref=src,
            dst_ref=dst,
            send_sem=a2a_sems.at[0, index],
            recv_sem=a2a_sems.at[1, index],
            device_id=(to_lon, to_lat),
            device_id_type=MESH,
        )

    def block(index):
        return pl.ds(aligned(index * 16, 16), 16)

    def along_lat(src, dst, base, k, incoming):
        peer = lax.rem(lat + (NLAT - k if incoming else k), NLAT)
        if incoming:
            return a2a(src.at[block(peer)], dst.at[block(peer)], base + k, lon, lat)
        return a2a(src.at[block(peer)], dst.at[block(lat)], base + k, lon, peer)

    def along_lon(src, dst, base, k, incoming):
        peer = lax.rem(lon + (NLON - k if incoming else k), NLON)
        if incoming:
            return a2a(src.at[block(peer)], dst.at[block(peer)], base + k, lon, lat)
        return a2a(src.at[block(peer)], dst.at[block(lon)], base + k, peer, lat)

    def start_hop(route, src, dst, base, count):
        loop(1, count, lambda k: route(src, dst, base, k, False).start())

    def end_hop(route, src, dst, base, count):
        def settle(k):
            route(src, dst, base, k, False).wait_send()
            route(src, dst, base, k, True).wait_recv()

        loop(1, count, settle)

    start_hop(along_lat, send_a, recv_a, 0, NLAT)
    recv_a[block(lat)] = send_a[block(lat)]

    normed = normalise(grid_ref[...].astype(F32))[0].astype(BF16)
    normed_ref[...] = normed
    queries = mm(normed, wq_ref[...]).astype(BF16)
    q_ref[...] = queries
    qt_ref[...] = queries.T
    mine = jnp.where(routes_ref[0] == me, 1.0, 0.0) + jnp.where(routes_ref[1] == me, 1.0, 0.0)
    counts = jnp.broadcast_to(jnp.sum(mine, axis=1, keepdims=True), (DEVICES, CH)).astype(BF16)
    slot = iota((256, DEVICES), 0)
    expand = one_hot((slot // 16) * NLAT + lax.rem(slot, NLAT) == iota((256, DEVICES), 1))
    rank = (lax.rem(iota((256, CH), 0), 16) // NLAT).astype(F32)
    live = jnp.where(mm(expand, counts) > rank + 0.5, 1.0, 0.0)
    live_ref[0:256] = live
    live_ref[256:512] = live
    for a in range(7):
        for b in range(7):
            tap = kernels_ref[a, b].astype(F32)
            for half in range(2):
                taps_ref[half, a * 7 + b] = tap[:, half * 128 : half * 128 + 128]

    out_row, in_row = iota((256, 256), 0), iota((256, 256), 1)
    shuffle = one_hot(
        (lax.rem(out_row, 16) // NLAT) * 128 + lax.rem(out_row, NLAT) * 16 + out_row // 16 == in_row
    )
    end_hop(along_lat, send_a, recv_a, 0, NLAT)
    send_b[...] = (
        mm(shuffle[:, :128], recv_a[:, :512]) + mm(shuffle[:, 128:], recv_a[:, 512:])
    ).astype(BF16)
    start_hop(along_lon, send_b, recv_b, 8, NLON)
    recv_b[block(lon)] = send_b[block(lon)]
    end_hop(along_lon, send_b, recv_b, 8, NLON)

    for token in range(2):
        tokens = recv_b[:, token * CH : token * CH + CH]
        rows = slice(token * 256, token * 256 + 256)
        k_ref[rows] = mm(tokens, wk_ref[...]).astype(BF16)
        v_ref[rows] = mm(tokens, wv_ref[...]).astype(BF16)
    kt_ref[...] = k_ref[...].T
    vt_ref[...] = v_ref[...].T

    def head_mask(head):
        return jnp.where(iota((1, CH), 1) // DEPTH == head, 1.0, 0.0).astype(BF16)

    def head_rows(head):
        return pl.ds(aligned(head * DEPTH, DEPTH), DEPTH)

    def attend(head):
        keys = k_ref[...] * head_mask(head)
        for part in range(2):
            cells = slice(part * 256, part * 256 + 256)
            raised = jnp.exp(mm(keys, qt_ref[:, cells]) * SCALE) * live_ref[...]
            weights = raised * (1.0 / jnp.sum(raised, axis=0, keepdims=True))
            probs = weights.astype(BF16)
            probs_ref[head, :, cells] = probs
            ctx_t_ref[head_rows(head), cells] = mm(vt_ref[head_rows(head), :], probs).astype(BF16)

    loop(0, HEADS, attend)

    state = (grid_ref[...].astype(F32) + mm_tn(ctx_t_ref[...], wo_ref[...])).astype(BF16)
    st_ref[0] = state.reshape(ROWS, COLS, CH)

    def halo(index, tile):
        return Halo(
            place,
            tile,
            halo_rows.at[index],
            halo_cols.at[index],
            halo_corners.at[index],
            halo_sems.at[index],
        )

    for layer in range(2):
        edge = halo(layer, st_ref.at[layer])
        edge.start()
        padded = pad_ref.at[layer]
        edge.fill_inner(padded)
        edge.fill_edges(padded)

        def store_mixed(half, chunk, sums):
            for row in range(ROWS):
                inner_ref[half, row, chunk * 16 : chunk * 16 + 16, :] = sums[row]

        correlate(padded, taps_ref, layer, False, store_mixed)

        def mix(row_pair):
            top = aligned(row_pair * 2, 2)
            mixed = jnp.concatenate(
                [inner_ref[0, pl.ds(top, 2)], inner_ref[1, pl.ds(top, 2)]], axis=-1
            ).reshape(128, CH)
            xhat, scale = normalise(mixed)
            rows = pl.ds(aligned(row_pair * 128, 128), 128)
            xhat_ref[layer, rows] = xhat
            rstd_ref[layer, rows] = jnp.broadcast_to(scale, (128, 128))
            normed_low = xhat.astype(BF16)
            nrm_ref[layer, rows] = normed_low
            pre = mm(normed_low, we_ref[layer])
            square = pre * pre
            curve = jnp.tanh(pre * (GELU_0 + GELU_1 * square))
            gate = 0.5 + 0.5 * curve
            wide = (pre * gate).astype(BF16)
            dgelu_ref[layer, rows] = gate + 0.5 * pre * (1.0 - curve * curve) * (
                GELU_0 + 3.0 * GELU_1 * square
            )
            wide_ref[layer, rows] = wide
            before_mix = st_ref[layer, pl.ds(top, 2)].reshape(128, CH).astype(F32)
            after = (before_mix + mm(wide, wr_ref[layer])).astype(BF16)
            if layer == 0:
                st_ref[1, pl.ds(top, 2)] = after.reshape(2, COLS, CH)
            else:
                analysis_ref[rows] = after

        loop(0, 4, mix)

    kgrad_ref[...] = jnp.zeros_like(kgrad_ref)
    reduce_1 = Exchange(place, x_1, half_1, l1_1, part_1, l2_1, out_1, sems_1, BIG)
    reduce_0 = Exchange(place, x_0, half_0, l1_0, part_0, l2_0, out_0, sems_0, BIG)
    reduce_att = Exchange(
        place, x_attention, half_att, l1_att, part_att, l2_att, out_attention, sems_att, BIG
    )
    reduce_k = SmallExchange(place, x_kernels, l1_k, part_k, l2_k, out_kernels, sems_k)

    grad_ref[...] = cot_ref[...].astype(F32)
    for layer in (1, 0):
        sums = x_1 if layer == 1 else x_0

        def unmix(row_pair):
            top = aligned(row_pair * 2, 2)
            rows = pl.ds(aligned(row_pair * 128, 128), 128)
            low = grad_ref[rows].astype(BF16)
            low_ref[rows] = low
            grad_pre = (mm_nt(low, wr_ref[layer]) * dgelu_ref[layer, rows]).astype(BF16)
            gpre_ref[rows] = grad_pre
            grad_norm = mm_nt(grad_pre, we_ref[layer])
            xhat = xhat_ref[layer, rows]
            centred = (
                grad_norm
                - jnp.mean(grad_norm, axis=-1, keepdims=True)
                - xhat * jnp.mean(grad_norm * xhat, axis=-1, keepdims=True)
            )
            grad_mixed = (centred * rstd_ref[layer, rows][:, :1]).astype(BF16)
            gl_ref[layer, pl.ds(top, 2)] = grad_mixed.reshape(2, COLS, CH)

        loop(0, 4, unmix)
        edge = halo(2 + layer, gl_ref.at[layer])
        edge.start()
        if layer == 0:
            reduce_1.start_2()
        edge.fill_inner(pad_back)

        for piece in range(4):
            lanes = slice(piece * 256, piece * 256 + 256)
            rows = slice(piece * 256, piece * 256 + 256)
            sums[rows] = mm_tn(nrm_ref[layer], gpre_ref[:, lanes]).astype(BF16)
            more = slice(1024 + piece * 256, 1280 + piece * 256)
            sums[more] = mm_tn(wide_ref[layer, :, lanes], low_ref[...]).astype(BF16)
        if layer == 1:
            reduce_1.start_0()
        else:
            reduce_1.start_3()
            reduce_0.start_0()

        for half in range(2):
            inner_ref[half] = pad_back[half, 3 : 3 + ROWS, 8 : 8 + COLS, :]
        kernel_grads(pad_ref.at[layer], inner_ref, kgrad_ref, layer)

        edge.fill_edges(pad_back)

        def add_direct(half, chunk, sums):
            for row in range(ROWS):
                inner_ref[half, row, chunk * 16 : chunk * 16 + 16, :] = sums[row]

        correlate(pad_back, taps_ref, layer, True, add_direct)
        for half in range(2):
            lanes = slice(half * 128, half * 128 + 128)
            grad_ref[:, lanes] = grad_ref[:, lanes] + inner_ref[half].reshape(CELLS, 128)
        if layer == 1:
            reduce_1.start_1()

    x_kernels[0:112, 0:128] = kgrad_ref[0].astype(BF16)
    x_kernels[0:112, 128:256] = kgrad_ref[1].astype(BF16)
    x_kernels[112:128] = jnp.zeros((16, CH), BF16)
    reduce_k.start_0()
    reduce_0.start_1()
    reduce_1.start_4()

    def put_attention(index, matrix):
        for half in range(2):
            row = (index * 2 + half) * 256
            x_attention[row : row + 256] = matrix[:, half * 128 : half * 128 + 128].astype(BF16)

    low = grad_ref[...].astype(BF16)
    put_attention(3, mm(ctx_t_ref[...], low))
    gctx = mm_nt(low, wo_ref[...]).astype(BF16)
    gctx_ref[...] = gctx
    gt_ref[...] = gctx.T
    dk_ref[...] = jnp.zeros_like(dk_ref)
    dv_ref[...] = jnp.zeros_like(dv_ref)

    def unattend(head):
        mask = head_mask(head)
        values = v_ref[...] * mask
        for part in range(2):
            cells = slice(part * 256, part * 256 + 256)
            probs = probs_ref[head, :, cells]
            weights = probs.astype(F32)
            grad_probs = mm(values, gt_ref[:, cells])
            mean = jnp.sum(weights * grad_probs, axis=0, keepdims=True)
            grad_scores = (weights * (grad_probs - mean)).astype(BF16)
            dv_ref[...] += mm(probs, gctx_ref[cells] * mask)
            dk_ref[...] += mm(grad_scores, q_ref[cells] * mask)
            dq_t_ref[head_rows(head), cells] = (
                mm(kt_ref[head_rows(head), :], grad_scores) * SCALE
            ).astype(BF16)

    loop(0, HEADS // 2, unattend)
    reduce_1.start_5()
    reduce_0.start_2()
    reduce_k.start_1()
    loop(HEADS // 2, HEADS, unattend)
    reduce_0.start_3()
    reduce_k.start_2()

    grad_keys = (dk_ref[...] * SCALE).astype(BF16)
    grad_values = dv_ref[...].astype(BF16)
    for token in range(2):
        rows = slice(token * 256, token * 256 + 256)
        back_b[:, token * CH : token * CH + CH] = (
            mm_nt(grad_keys[rows], wk_ref[...]) + mm_nt(grad_values[rows], wv_ref[...])
        ).astype(BF16)
    start_hop(along_lon, back_b, got_b, 24, NLON)
    got_b[block(lon)] = back_b[block(lon)]

    put_attention(0, mm(dq_t_ref[...], normed_ref[...]).T)
    for index, grads in ((1, grad_keys), (2, grad_values)):
        put_attention(
            index,
            mm_tn(recv_b[:, :CH], grads[:256]) + mm_tn(recv_b[:, CH:], grads[256:]),
        )
    reduce_att.start_0()
    reduce_0.start_4()

    end_hop(along_lon, back_b, got_b, 24, NLON)
    for c in range(2):
        back_a[:, c * 512 : c * 512 + 512] = mm_tn(
            shuffle[:, c * 128 : c * 128 + 128], got_b[...]
        ).astype(BF16)
    start_hop(along_lat, back_a, got_a, 40, NLAT)
    got_a[block(lat)] = back_a[block(lat)]
    reduce_att.start_1()
    reduce_0.start_5()
    reduce_k.finish()
    end_hop(along_lat, back_a, got_a, 40, NLAT)
    grad_enc_ref[...] = mm_tn(chosen_ref[0], got_a[:, :512]) + mm_tn(chosen_ref[1], got_a[:, 512:])
    reduce_att.start_2()
    reduce_1.finish()
    reduce_att.start_3()
    reduce_0.finish()
    reduce_att.start_4()
    reduce_att.start_5()
    reduce_att.finish()


def fused(*operands):
    vm = pl.BlockSpec(memory_space=pltpu.VMEM)

    def b(*shape):
        return pltpu.VMEM(shape, BF16)

    def f(*shape):
        return pltpu.VMEM(shape, F32)

    def sem(*shape):
        return pltpu.SemaphoreType.DMA(shape)

    scratch = [
        b(2, DEVICES, BLOCKS_DEV),
        b(128, 1024),
        b(128, 1024),
        b(256, 512),
        b(256, 512),
        b(256, 512),
        b(256, 512),
        b(128, 1024),
        b(128, 1024),
        f(SLOTS, 256),
        b(CELLS, CH),
        b(CELLS, CH),
        b(CH, CELLS),
        b(SLOTS, CH),
        b(CH, SLOTS),
        b(SLOTS, CH),
        b(CH, SLOTS),
        b(HEADS, SLOTS, CELLS),
        b(CH, CELLS),
        b(2, ROWS, COLS, CH),
        b(2, ROWS, COLS, CH),
        f(2, 2, PAD_ROWS, PAD_COLS, 128),
        f(2, PAD_ROWS, PAD_COLS, 128),
        f(2, ROWS, COLS, 128),
        f(2, 49, 2, 128),
        f(2, 112, 128),
        f(2, CELLS, CH),
        f(2, CELLS, 128),
        b(2, CELLS, CH),
        b(2, CELLS, WIDE),
        f(2, CELLS, WIDE),
        b(CELLS, WIDE),
        f(CELLS, CH),
        b(CELLS, CH),
        b(CELLS, CH),
        b(CH, CELLS),
        b(CH, CELLS),
        f(SLOTS, CH),
        f(SLOTS, CH),
        b(4, 2, 3, COLS, CH),
        b(4, 2, ROWS, 16, CH),
        b(4, 4, 3, 16, CH),
        b(BIG, 128),
        b(KROWS, CH),
        b(BIG, CH),
        b(BIG, CH),
        b(BIG // 2, 128),
        b(BIG // 2, CH),
        b(BIG // 2, CH),
        b(NLAT, BIG // 16, 128),
        b(NLAT, BIG // 16, CH),
        b(NLAT, BIG // 16, CH),
        b(BIG // 16, 128),
        b(BIG // 16, CH),
        b(BIG // 16, CH),
        b(NYZ, BIG // 128, 128),
        b(NYZ, BIG // 128, CH),
        b(NYZ, BIG // 128, CH),
        b(NLAT, 16, CH),
        b(16, CH),
        b(NLON, 16, CH),
        sem(2, 48),
        sem(4, 2, 8),
        sem(2, 32),
        sem(2, 32),
        sem(2, 32),
        sem(2, 32),
    ]
    return pl.pallas_call(
        kernel,
        out_shape=[
            jax.ShapeDtypeStruct((CELLS, CH), BF16),
            jax.ShapeDtypeStruct((BLOCKS_DEV, 512), F32),
            jax.ShapeDtypeStruct((BIG, 128), BF16),
            jax.ShapeDtypeStruct((KROWS, CH), BF16),
            jax.ShapeDtypeStruct((BIG, CH), BF16),
            jax.ShapeDtypeStruct((BIG, CH), BF16),
        ],
        in_specs=[vm] * len(operands),
        out_specs=[vm] * 6,
        scratch_shapes=scratch,
        compiler_params=pltpu.CompilerParams(
            collective_id=0, has_side_effects=True, vmem_limit_bytes=56 * 1024 * 1024
        ),
        name="assimilate",
    )(*operands)


def local(
    grid_state,
    encodings,
    routes,
    w_query,
    w_key,
    w_value,
    w_out,
    kernels,
    w_expand,
    w_reduce,
    cotangent,
):
    analysis, grad_enc, attention, taps, sums_1, sums_0 = fused(
        grid_state.reshape(CELLS, CH),
        encodings.reshape(BLOCKS_DEV, 2 * CH),
        routes.T.reshape(2, DEVICES, BLOCKS_DEV),
        w_query,
        w_key,
        w_value,
        w_out,
        kernels.transpose(1, 2, 0, 3),
        w_expand,
        w_reduce,
        cotangent.reshape(CELLS, CH),
    )
    attention = attention.astype(F32).reshape(4, 2, CH, 128).transpose(0, 2, 1, 3)
    taps = taps[:112].astype(F32).reshape(2, 56, CH)[:, :49].reshape(2, 7, 7, CH)
    both = jnp.stack([sums_0, sums_1]).astype(F32)
    expand = both[:, :1024].reshape(2, 4, CH, CH).transpose(0, 2, 1, 3).reshape(2, CH, WIDE)
    reduce = both[:, 1024:]
    return (
        analysis.reshape(ROWS, COLS, CH),
        grad_enc.reshape(BLOCKS_DEV, 2, CH),
        attention.reshape(4, CH, CH),
        taps,
        expand,
        reduce,
    )


def solution(mesh):
    in_specs = (
        P("lat", "lon", None),
        P(("lon", "lat"), None, None),
        P(),
        P(),
        P(),
        P(),
        P(),
        P(),
        P(),
        P(),
        P("lat", "lon", None),
    )
    out_specs = (P("lat", "lon", None), P(("lon", "lat"), None, None), P(), P(), P(), P())
    return jax.shard_map(local, mesh=mesh, in_specs=in_specs, out_specs=out_specs, check_vma=False)
```

profile of v0, /device:TPU:1, one launch (start us, length us, event | category | flops | bytes accessed | tf_op | source)
XLA Modules:
  0.0 163.6 jit_solution(2265360023508235437)
XLA Ops:
  0.6 1.7 %reshape.58.routes_ref = s32[2,128,96]{2,1,0:T(8,128)} reshape(s32[2,12288]{1,0:T(2,128)} %bitcast.35) | data formatting | bytes 196608 | tf_op jit(solution)/shard_map/reshape | solution.py:931
  2.3 1.5 copy.25
  3.9 151.3 %assimilate.1 = (bf16[512,256]{1,0:T(8,128)(2,1)}, f32[96,512]{1,0:T(8,128)}, bf16[2048,128]{1,0:T(8,128)(2,1)}, bf16[128,256]{1,0:T(8,128)(2,1)}, bf16[2048,256]{1,0:T(8,128)(2,1)}, /*index=5*/bf16[2048,256]{1,0:T(8,128)(2,1)}) custom-call(bf16[512,256]{1,0:T(8,128)(2,1)} %bitcast.30, bf16[96,512]{1,0:T(8,128)(2,1)} %bitcast.29, ...), custom_call_target="tpu_custom_call" | custom-call | tf_op jit(solution)/shard_map/assimilate/pallas_call | solution.py:895
  155.2 1.8 %maximum_convert_fusion = f32[2,2048,256]{2,1,0:T(8,128)S(1)} fusion(bf16[1,2048,256]{2,1,0:T(8,128)(2,1)} %bitcast.26, bf16[1,2048,256]{2,1,0:T(8,128)(2,1)} %bitcast.27), kind=kLoop, calls=%fused_computation | loop fusion | flops 2097152 | bytes 6291456 | tf_op jit(solution)/shard_map/convert_element_type | solution.py:943
  157.0 1.7 %fusion = (f32[2,1024,256]{2,1,0:T(8,128)}, f32[2,1024,256]{2,1,0:T(8,128)S(1)}) fusion(f32[2,2048,256]{2,1,0:T(8,128)S(1)} %maximum_convert_fusion), kind=kLoop, calls=%fused_computation.4 | loop fusion | bytes 8388608 | tf_op jit(solution)/shard_map/slice | solution.py:945
  158.7 0.0 copy-start
  158.7 0.0 copy-start.3
  158.7 0.0 copy-start.2
  158.7 1.6 copy.24
  160.3 0.0 copy-start.1
  160.3 0.0 copy-done
  160.3 1.1 copy_bitcast_fusion
  161.4 0.0 copy-done.3
  161.4 0.7 copy.21
  162.1 0.0 copy-done.2
  162.1 0.8 reshape.61
  162.9 0.0 copy-done.1
  162.9 0.7 copy.28
  (2 shorter events, 0.0 us)
Async XLA Ops:
  158.7 1.6 %copy-start = (bf16[2048,128]{1,0:T(8,128)(2,1)S(1)}, bf16[2048,128]{1,0:T(8,128)(2,1)}, u32[]{:S(2)}) copy-start(bf16[2048,128]{1,0:T(8,128)(2,1)} %get-tuple-element.14) | copy-start | bytes 1572868
  158.7 2.7 %copy-start.3 = (bf16[128,256]{1,0:T(8,128)(2,1)S(1)}, bf16[128,256]{1,0:T(8,128)(2,1)}, u32[]{:S(2)}) copy-start(bf16[128,256]{1,0:T(8,128)(2,1)} %get-tuple-element.15) | copy-start | bytes 196612
  158.7 3.4 %copy-start.2 = (f32[96,512]{1,0:T(8,128)S(1)}, f32[96,512]{1,0:T(8,128)}, u32[]{:S(2)}) copy-start(f32[96,512]{1,0:T(8,128)} %get-tuple-element.13) | copy-start | bytes 589828
  160.3 2.6 %copy-start.1 = (bf16[512,256]{1,0:T(8,128)(2,1)S(1)}, bf16[512,256]{1,0:T(8,128)(2,1)}, u32[]{:S(2)}) copy-start(bf16[512,256]{1,0:T(8,128)(2,1)} %get-tuple-element.12) | copy-start | bytes 786436
where the time goes:
time: 164 us
  Pallas kernels  151 us (92%)
  local copies, waits for them, and re-layouts  8.8 us (5%)
  other arithmetic  2.88 us (2%)
    pallas_call x1, Pallas kernels, fused(): pl.pallas_call(kernel, out_shape=[jax.ShapeDtypeStruct((CELLS, CH), BF16)...  151 us

commit v1 on v0

--- a/solution.py
+++ b/solution.py
@@ -60,12 +60,168 @@
 
 
 class Exchange:
-    def __init__(self, place, source, half, level_1, part, level_2, total, sems, rows):
+    def __init__(
+        self, place, lat_first, whole, source, half, level_1, part, level_2, total, sems, rows
+    ):
         self.lon, self.lat, self.core, self.yz = place
+        self.lat_first, self.whole = lat_first, whole
+        self.first, self.second = (self.lat, self.yz) if lat_first else (self.yz, self.lat)
         self.source, self.half, self.level_1 = source, half, level_1
         self.part, self.level_2, self.total = part, level_2, total
         self.sems = sems
         self.r1, self.r2, self.r3 = rows // 2, rows // 16, rows // 128
+
+    def copy(self, src, dst, index, device):
+        return pltpu.make_async_remote_copy(
+            src_ref=src,
+            dst_ref=dst,
+            send_sem=self.sems.at[0, index],
+            recv_sem=self.sems.at[1, index],
+            device_id=device,
+            device_id_type=MESH,
+        )
+
+    def pair(self):
+        return (self.lon + 1 - 2 * self.core, self.lat)
+
+    def device(self, on_lat, position):
+        if on_lat:
+            return (self.lon, position)
+        return (position * 2 + self.core, self.lat)
+
+    def to_first(self, k):
+        return lax.rem(self.first + k, 8)
+
+    def from_first(self, k):
+        return lax.rem(self.first + 8 - k, 8)
+
+    def to_second(self, k):
+        return lax.rem(self.second + k, 8)
+
+    def from_second(self, k):
+        return lax.rem(self.second + 8 - k, 8)
+
+    def copy_0(self):
+        other = aligned((1 - self.core) * self.r1, self.r1)
+        return self.copy(self.source.at[pl.ds(other, self.r1)], self.half, 0, self.pair())
+
+    def start_0(self):
+        self.copy_0().start()
+
+    def copy_1(self, k):
+        peer = self.to_first(k)
+        return self.copy(
+            self.half.at[pl.ds(aligned(peer * self.r2, self.r2), self.r2)],
+            self.level_1.at[k],
+            k,
+            self.device(self.lat_first, peer),
+        )
+
+    def start_1(self):
+        self.copy_0().wait()
+        mine = aligned(self.core * self.r1, self.r1)
+        step = self.r1 // 4
+
+        def add(i):
+            at = aligned(i * step, step)
+            self.half[pl.ds(at, step)] = (
+                self.half[pl.ds(at, step)].astype(F32)
+                + self.source[pl.ds(aligned(mine + at, step), step)].astype(F32)
+            ).astype(BF16)
+
+        loop(0, 4, add)
+        loop(1, 8, lambda k: self.copy_1(k).start())
+
+    def copy_2(self, k):
+        peer = self.to_second(k)
+        device = self.device(not self.lat_first, peer)
+        if self.whole:
+            return self.copy(self.part, self.level_2.at[k], 8 + k, device)
+        return self.copy(
+            self.part.at[pl.ds(aligned(peer * self.r3, self.r3), self.r3)],
+            self.level_2.at[k],
+            8 + k,
+            device,
+        )
+
+    def start_2(self):
+        loop(1, 8, lambda k: self.copy_1(k).wait())
+        total = self.half[pl.ds(aligned(self.first * self.r2, self.r2), self.r2)].astype(F32)
+        for k in range(1, 8):
+            total = total + self.level_1[k].astype(F32)
+        self.part[...] = total.astype(BF16)
+        loop(1, 8, lambda k: self.copy_2(k).start())
+
+    def offset(self, first, second):
+        return self.core * self.r1 + first * self.r2 + second * self.r3
+
+    def copy_3(self, k):
+        rows = pl.ds(aligned(self.offset(self.first, self.second), self.r3), self.r3)
+        device = self.device(not self.lat_first, self.to_second(k))
+        return self.copy(self.total.at[rows], self.total.at[rows], 16 + k, device)
+
+    def start_3(self):
+        loop(1, 8, lambda k: self.copy_2(k).wait())
+        if self.whole:
+            self.level_2[0] = self.part[...]
+            total = jnp.zeros(self.part.shape, F32)
+            for index in range(8):
+                total = total + self.level_2[lax.rem(self.second + 8 - index, 8)].astype(F32)
+            rows = pl.ds(aligned(self.offset(self.first, 0), self.r2), self.r2)
+            self.total[rows] = total.astype(BF16)
+            loop(1, 8, lambda k: self.copy_4(k).start())
+            return
+        total = self.part[pl.ds(aligned(self.second * self.r3, self.r3), self.r3)].astype(F32)
+        for k in range(1, 8):
+            total = total + self.level_2[k].astype(F32)
+        rows = pl.ds(aligned(self.offset(self.first, self.second), self.r3), self.r3)
+        self.total[rows] = total.astype(BF16)
+        loop(1, 8, lambda k: self.copy_3(k).start())
+
+    def copy_4(self, k):
+        rows = pl.ds(aligned(self.offset(self.first, 0), self.r2), self.r2)
+        device = self.device(self.lat_first, self.to_first(k))
+        return self.copy(self.total.at[rows], self.total.at[rows], 24 + k, device)
+
+    def start_4(self):
+        def settle(k):
+            self.copy_3(k).wait_send()
+            rows = pl.ds(aligned(self.offset(self.first, self.from_second(k)), self.r3), self.r3)
+            self.copy(
+                self.total.at[rows], self.total.at[rows], 16 + k, (self.lon, self.lat)
+            ).wait_recv()
+
+        loop(1, 8, settle)
+        loop(1, 8, lambda k: self.copy_4(k).start())
+
+    def copy_5(self):
+        rows = pl.ds(aligned(self.core * self.r1, self.r1), self.r1)
+        return self.copy(self.total.at[rows], self.total.at[rows], 8, self.pair())
+
+    def start_5(self):
+        def settle(k):
+            self.copy_4(k).wait_send()
+            rows = pl.ds(aligned(self.offset(self.from_first(k), 0), self.r2), self.r2)
+            self.copy(
+                self.total.at[rows], self.total.at[rows], 24 + k, (self.lon, self.lat)
+            ).wait_recv()
+
+        loop(1, 8, settle)
+        self.copy_5().start()
+
+    def finish(self):
+        self.copy_5().wait_send()
+        rows = pl.ds(aligned((1 - self.core) * self.r1, self.r1), self.r1)
+        self.copy(
+            self.total.at[rows], self.total.at[rows], 8, (self.lon, self.lat)
+        ).wait_recv()
+
+
+class SmallExchange:
+    def __init__(self, place, source, level_1, part, level_2, total, sems):
+        self.lon, self.lat, self.core, self.yz = place
+        self.source, self.level_1, self.part = source, level_1, part
+        self.level_2, self.total, self.sems = level_2, total, sems
 
     def copy(self, src, dst, index, lon, lat):
         return pltpu.make_async_remote_copy(
@@ -77,153 +233,6 @@
             device_id_type=MESH,
         )
 
-    def pair(self):
-        return self.lon + 1 - 2 * self.core
-
-    def lat_peer(self, k):
-        return lax.rem(self.lat + k, NLAT)
-
-    def lat_from(self, k):
-        return lax.rem(self.lat + NLAT - k, NLAT)
-
-    def yz_peer(self, k):
-        return lax.rem(self.yz + k, NYZ)
-
-    def yz_from(self, k):
-        return lax.rem(self.yz + NYZ - k, NYZ)
-
-    def copy_0(self):
-        other = aligned((1 - self.core) * self.r1, self.r1)
-        return self.copy(
-            self.source.at[pl.ds(other, self.r1)], self.half.at[...], 0, self.pair(), self.lat
-        )
-
-    def start_0(self):
-        self.copy_0().start()
-
-    def copy_1(self, k):
-        peer = self.lat_peer(k)
-        return self.copy(
-            self.half.at[pl.ds(aligned(peer * self.r2, self.r2), self.r2)],
-            self.level_1.at[k],
-            k,
-            self.lon,
-            peer,
-        )
-
-    def start_1(self):
-        self.copy_0().wait()
-        mine = aligned(self.core * self.r1, self.r1)
-        step = self.r1 // 4
-
-        def add(i):
-            at = aligned(i * step, step)
-            self.half[pl.ds(at, step)] = (
-                self.half[pl.ds(at, step)].astype(F32)
-                + self.source[pl.ds(aligned(mine + at, step), step)].astype(F32)
-            ).astype(BF16)
-
-        loop(0, 4, add)
-        loop(1, NLAT, lambda k: self.copy_1(k).start())
-
-    def copy_2(self, k):
-        peer = self.yz_peer(k)
-        return self.copy(
-            self.part.at[pl.ds(aligned(peer * self.r3, self.r3), self.r3)],
-            self.level_2.at[k],
-            8 + k,
-            peer * 2 + self.core,
-            self.lat,
-        )
-
-    def start_2(self):
-        loop(1, NLAT, lambda k: self.copy_1(k).wait())
-        total = self.half[pl.ds(aligned(self.lat * self.r2, self.r2), self.r2)].astype(F32)
-        for k in range(1, NLAT):
-            total = total + self.level_1[k].astype(F32)
-        self.part[...] = total.astype(BF16)
-        loop(1, NYZ, lambda k: self.copy_2(k).start())
-
-    def offset(self, core, lat, yz):
-        return core * self.r1 + lat * self.r2 + yz * self.r3
-
-    def copy_3(self, k):
-        rows = pl.ds(aligned(self.offset(self.core, self.lat, self.yz), self.r3), self.r3)
-        return self.copy(
-            self.total.at[rows],
-            self.total.at[rows],
-            16 + k,
-            self.yz_peer(k) * 2 + self.core,
-            self.lat,
-        )
-
-    def start_3(self):
-        loop(1, NYZ, lambda k: self.copy_2(k).wait())
-        total = self.part[pl.ds(aligned(self.yz * self.r3, self.r3), self.r3)].astype(F32)
-        for k in range(1, NYZ):
-            total = total + self.level_2[k].astype(F32)
-        rows = pl.ds(aligned(self.offset(self.core, self.lat, self.yz), self.r3), self.r3)
-        self.total[rows] = total.astype(BF16)
-        loop(1, NYZ, lambda k: self.copy_3(k).start())
-
-    def copy_4(self, k):
-        rows = pl.ds(aligned(self.offset(self.core, self.lat, 0), self.r2), self.r2)
-        return self.copy(
-            self.total.at[rows], self.total.at[rows], 24 + k, self.lon, self.lat_peer(k)
-        )
-
-    def start_4(self):
-        def settle(k):
-            self.copy_3(k).wait_send()
-            rows = pl.ds(
-                aligned(self.offset(self.core, self.lat, self.yz_from(k)), self.r3), self.r3
-            )
-            self.copy(
-                self.total.at[rows], self.total.at[rows], 16 + k, self.lon, self.lat
-            ).wait_recv()
-
-        loop(1, NYZ, settle)
-        loop(1, NLAT, lambda k: self.copy_4(k).start())
-
-    def copy_5(self):
-        rows = pl.ds(aligned(self.core * self.r1, self.r1), self.r1)
-        return self.copy(self.total.at[rows], self.total.at[rows], 8, self.pair(), self.lat)
-
-    def start_5(self):
-        def settle(k):
-            self.copy_4(k).wait_send()
-            rows = pl.ds(aligned(self.offset(self.core, self.lat_from(k), 0), self.r2), self.r2)
-            self.copy(
-                self.total.at[rows], self.total.at[rows], 24 + k, self.lon, self.lat
-            ).wait_recv()
-
-        loop(1, NLAT, settle)
-        self.copy_5().start()
-
-    def finish(self):
-        self.copy_5().wait_send()
-        rows = pl.ds(aligned((1 - self.core) * self.r1, self.r1), self.r1)
-        self.copy(
-            self.total.at[rows], self.total.at[rows], 8, self.lon, self.lat
-        ).wait_recv()
-
-
-class SmallExchange:
-    def __init__(self, place, source, level_1, part, level_2, total, sems):
-        self.lon, self.lat, self.core, self.yz = place
-        self.source, self.level_1, self.part = source, level_1, part
-        self.level_2, self.total, self.sems = level_2, total, sems
-
-    def copy(self, src, dst, index, lon, lat):
-        return pltpu.make_async_remote_copy(
-            src_ref=src,
-            dst_ref=dst,
-            send_sem=self.sems.at[0, index],
-            recv_sem=self.sems.at[1, index],
-            device_id=(lon, lat),
-            device_id_type=MESH,
-        )
-
     def copy_0(self, k):
         peer = lax.rem(self.lat + k, NLAT)
         return self.copy(
@@ -272,39 +281,46 @@
 
 
 class Halo:
-    def __init__(self, place, tile, rows, cols, corners, sems):
+    def __init__(self, place, tile, packed, rows, cols, corners, sems):
         self.lon, self.lat = place[0], place[1]
-        self.tile, self.rows, self.cols, self.corners, self.sems = tile, rows, cols, corners, sems
-
-    def copies(self):
+        self.tile, self.packed, self.rows = tile, packed, rows
+        self.cols, self.corners, self.sems = cols, corners, sems
+
+    def copies(self, wanted=range(8)):
         east, west = lax.rem(self.lon + 1, NLON), lax.rem(self.lon + NLON - 1, NLON)
         south, north = lax.rem(self.lat + 1, NLAT), lax.rem(self.lat + NLAT - 1, NLAT)
-        top, bottom, whole = pl.ds(0, 3), pl.ds(ROWS - 3, 3), pl.ds(0, ROWS)
-        left, right, wide = pl.ds(0, 16), pl.ds(COLS - 16, 16), pl.ds(0, COLS)
+        upper, lower = pl.ds(0, 16), pl.ds(16, 16)
         plan = [
-            (top, wide, self.rows.at[1], self.lon, north),
-            (bottom, wide, self.rows.at[0], self.lon, south),
-            (whole, left, self.cols.at[1], west, self.lat),
-            (whole, right, self.cols.at[0], east, self.lat),
-            (top, left, self.corners.at[3], west, north),
-            (top, right, self.corners.at[2], east, north),
-            (bottom, left, self.corners.at[1], west, south),
-            (bottom, right, self.corners.at[0], east, south),
+            (self.tile.at[pl.ds(0, 3)], self.rows.at[1], self.lon, north),
+            (self.tile.at[pl.ds(ROWS - 3, 3)], self.rows.at[0], self.lon, south),
+            (self.packed.at[0], self.cols.at[1], west, self.lat),
+            (self.packed.at[1], self.cols.at[0], east, self.lat),
+            (self.packed.at[0, upper], self.corners.at[3], west, north),
+            (self.packed.at[1, upper], self.corners.at[2], east, north),
+            (self.packed.at[0, lower], self.corners.at[1], west, south),
+            (self.packed.at[1, lower], self.corners.at[0], east, south),
         ]
         return [
             pltpu.make_async_remote_copy(
-                src_ref=self.tile.at[r, c],
+                src_ref=src,
                 dst_ref=dst,
                 send_sem=self.sems.at[0, index],
                 recv_sem=self.sems.at[1, index],
                 device_id=(lon, lat),
                 device_id_type=MESH,
             )
-            for index, (r, c, dst, lon, lat) in enumerate(plan)
+            for index, (src, dst, lon, lat) in enumerate(plan)
+            if index in wanted
         ]
 
     def start(self):
-        for copy in self.copies():
+        for copy in self.copies((0, 1)):
+            copy.start()
+        first = [self.tile[row, 0:16, :].astype(F32)[0:4] for row in range(ROWS)]
+        last = [self.tile[row, COLS - 16 : COLS, :].astype(F32)[12:16] for row in range(ROWS)]
+        self.packed[0] = jnp.concatenate(first, axis=0).astype(BF16)
+        self.packed[1] = jnp.concatenate(last, axis=0).astype(BF16)
+        for copy in self.copies(range(2, 8)):
             copy.start()
 
     def fill_inner(self, padded):
@@ -313,45 +329,55 @@
             for half in range(2):
                 padded[half, 3 + row, 8 : 8 + COLS, :] = cells[:, half * 128 : half * 128 + 128]
 
-    def fill_edges(self, padded):
-        for copy in self.copies():
+    def fill_sides(self, padded):
+        for copy in self.copies((2, 3)):
+            copy.wait()
+        for side, col in ((0, 4), (1, 8 + COLS)):
+            cells = self.cols[side].astype(F32)
+            for row in range(ROWS):
+                for half in range(2):
+                    padded[half, 3 + row, col : col + 4, :] = cells[
+                        row * 4 : row * 4 + 4, half * 128 : half * 128 + 128
+                    ]
+
+    def fill_ends(self, padded):
+        for copy in self.copies((0, 1, 4, 5, 6, 7)):
             copy.wait()
         has_north = jnp.where(self.lat > 0, 1.0, 0.0).astype(F32)
         has_south = jnp.where(self.lat < NLAT - 1, 1.0, 0.0).astype(F32)
-        for half in range(2):
-            lanes = slice(half * 128, half * 128 + 128)
-            for row in range(ROWS):
-                padded[half, 3 + row, 0:8, :] = self.cols[0, row, 8:16, lanes].astype(F32)
-                padded[half, 3 + row, 72:80, :] = self.cols[1, row, 0:8, lanes].astype(F32)
+        for end, there, start, skip in ((0, has_north, 0, 1), (1, has_south, 3 + ROWS, 0)):
+            corners = [self.corners[2 * end + side].astype(F32) * there for side in range(2)]
             for row in range(3):
-                for side, there, start in ((0, has_north, 0), (1, has_south, 3 + ROWS)):
-                    padded[half, start + row, 8 : 8 + COLS, :] = (
-                        self.rows[side, row, :, lanes].astype(F32) * there
-                    )
-                    padded[half, start + row, 0:8, :] = (
-                        self.corners[2 * side, row, 8:16, lanes].astype(F32) * there
-                    )
-                    padded[half, start + row, 72:80, :] = (
-                        self.corners[2 * side + 1, row, 0:8, lanes].astype(F32) * there
-                    )
-
-
-def correlate(padded, taps, block, flipped, store):
+                cells = self.rows[end, row].astype(F32) * there
+                at = (row + skip) * 4
+                for half in range(2):
+                    lanes = slice(half * 128, half * 128 + 128)
+                    padded[half, start + row, 8 : 8 + COLS, :] = cells[:, lanes]
+                    padded[half, start + row, 4:8, :] = corners[0][at : at + 4, lanes]
+                    padded[half, start + row, 8 + COLS : 12 + COLS, :] = corners[1][at : at + 4, lanes]
+
+
+def correlate(padded, taps, block, flipped, inside, result, chunks):
     def one_half(half):
-        for chunk in range(4):
-            sums = [None] * ROWS
+        for chunk in chunks:
+            cols = slice(chunk * 16, chunk * 16 + 16)
+            sums = [None if inside else result[half, row, cols, :] for row in range(ROWS)]
             for b in range(7):
-                rows = [
-                    padded[half, row, chunk * 16 + b + 5 : chunk * 16 + b + 21, :]
-                    for row in range(PAD_ROWS)
-                ]
+                rows = {}
                 for a in range(7):
                     tap_id = (6 - a) * 7 + (6 - b) if flipped else a * 7 + b
                     tap = taps[half, tap_id, block : block + 1, :]
                     for row in range(ROWS):
+                        if (3 <= row + a < 3 + ROWS) != inside:
+                            continue
+                        if row + a not in rows:
+                            first = chunk * 16 + b + 5
+                            rows[row + a] = padded[half, row + a, first : first + 16, :]
                         term = rows[row + a] * tap
                         sums[row] = term if sums[row] is None else sums[row] + term
-            store(half, chunk, sums)
+            for row in range(ROWS):
+                if inside or row < 3 or row >= ROWS - 3:
+                    result[half, row, cols, :] = sums[row]
 
     loop(0, 2, one_half)
 
@@ -373,7 +399,7 @@
                         term = rows[row + a] * grads[row]
                         sums[a] = term if sums[a] is None else sums[a] + term
             for a in range(7):
-                results[half, pl.ds(block * 56 + a * 7 + b, 1), :] = jnp.sum(
+                results[half, pl.ds((a * 7 + b) * 2 + block, 1), :] = jnp.sum(
                     sums[a], axis=0, keepdims=True
                 )
 
@@ -396,6 +422,23 @@
 
 
 def kernel(
+    grid_hbm,
+    enc_hbm,
+    routes_hbm,
+    wq_hbm,
+    wk_hbm,
+    wv_hbm,
+    wo_hbm,
+    kernels_hbm,
+    we_hbm,
+    wr_hbm,
+    cot_hbm,
+    analysis_ref,
+    grad_enc_ref,
+    out_attention,
+    out_kernels,
+    out_1,
+    out_0,
     grid_ref,
     enc_ref,
     routes_ref,
@@ -407,12 +450,7 @@
     we_ref,
     wr_ref,
     cot_ref,
-    analysis_ref,
-    grad_enc_ref,
-    out_attention,
-    out_kernels,
-    out_1,
-    out_0,
+    load_sems,
     chosen_ref,
     send_a,
     recv_a,
@@ -423,6 +461,7 @@
     back_a,
     got_a,
     live_ref,
+    group_ref,
     normed_ref,
     q_ref,
     qt_ref,
@@ -452,6 +491,7 @@
     dq_t_ref,
     dk_ref,
     dv_ref,
+    halo_packed,
     halo_rows,
     halo_cols,
     halo_corners,
@@ -486,6 +526,26 @@
     place = (lon, lat, core, yz)
     me = lon * NLAT + lat
 
+    pairs = (
+        (routes_hbm, routes_ref),
+        (enc_hbm, enc_ref),
+        (grid_hbm, grid_ref),
+        (wq_hbm, wq_ref),
+        (kernels_hbm, kernels_ref),
+        (wk_hbm, wk_ref),
+        (wv_hbm, wv_ref),
+        (wo_hbm, wo_ref),
+        (we_hbm, we_ref),
+        (wr_hbm, wr_ref),
+        (cot_hbm, cot_ref),
+    )
+    loads = [
+        pltpu.make_async_copy(source, target, load_sems.at[index])
+        for index, (source, target) in enumerate(pairs)
+    ]
+    for load in loads:
+        load.start()
+
     barrier = pltpu.get_barrier_semaphore()
 
     def greet(to_lon, to_lat):
@@ -497,18 +557,26 @@
         for dy in (1, NLAT - 1):
             greet(lax.rem(lon + dx, NLON), lax.rem(lat + dy, NLAT))
 
+    loads[0].wait()
+    loads[1].wait()
+    chunk = jnp.minimum(me * BLOCKS_DEV // 128, DEVICES * BLOCKS_DEV // 128 - 2)
+    shift = me * BLOCKS_DEV - chunk * 128
+    window = routes_ref[:, pl.ds(aligned(chunk * 128, 128), 256)].astype(F32).astype(BF16)
+    pick = one_hot(iota((256, BLOCKS_DEV), 0) == iota((256, BLOCKS_DEV), 1) + shift)
+    own = mm(window, pick).astype(jnp.int32)
     row_id = iota((DEVICES, BLOCKS_DEV), 0)
     tile_id = lax.rem(row_id, NLON) * NLAT + row_id // NLON
-    hits = (routes_ref[0, pl.ds(me, 1), :] == tile_id) | (
-        routes_ref[1, pl.ds(me, 1), :] == tile_id
-    )
+    hits = (own[0:1] == tile_id) | (own[1:2] == tile_id)
     before = one_hot(iota((BLOCKS_DEV, BLOCKS_DEV), 0) < iota((BLOCKS_DEV, BLOCKS_DEV), 1))
     hot = one_hot(hits)
     earlier = mm(hot, before)
+    tokens_f32 = enc_ref[...].astype(F32)
     for c in range(2):
         chosen = jnp.where(jnp.abs(earlier - c) < 0.5, hot.astype(F32), 0.0).astype(BF16)
         chosen_ref[c] = chosen
-        send_a[:, c * 512 : c * 512 + 512] = mm(chosen, enc_ref[...]).astype(BF16)
+        for token in range(2):
+            at = c * 512 + token * CH
+            send_a[:, at : at + CH] = mm(chosen, tokens_f32[:, token, :].astype(BF16)).astype(BF16)
 
     pl.semaphore_wait(barrier, NLAT - 1 + NLON - 1 + 4)
 
@@ -550,19 +618,31 @@
     start_hop(along_lat, send_a, recv_a, 0, NLAT)
     recv_a[block(lat)] = send_a[block(lat)]
 
+    loads[2].wait()
+    loads[3].wait()
     normed = normalise(grid_ref[...].astype(F32))[0].astype(BF16)
     normed_ref[...] = normed
     queries = mm(normed, wq_ref[...]).astype(BF16)
     q_ref[...] = queries
     qt_ref[...] = queries.T
-    mine = jnp.where(routes_ref[0] == me, 1.0, 0.0) + jnp.where(routes_ref[1] == me, 1.0, 0.0)
-    counts = jnp.broadcast_to(jnp.sum(mine, axis=1, keepdims=True), (DEVICES, CH)).astype(BF16)
-    slot = iota((256, DEVICES), 0)
-    expand = one_hot((slot // 16) * NLAT + lax.rem(slot, NLAT) == iota((256, DEVICES), 1))
+    mine = jnp.sum(jnp.where(routes_ref[...] == me, 1.0, 0.0), axis=0, keepdims=True)
+    for group in range(32):
+        group_ref[group : group + 1, :] = mine[:, group * 384 : group * 384 + 384]
+    fold = one_hot(iota((384, 128), 0) // BLOCKS_DEV == iota((384, 128), 1))
+    counts = mm(group_ref[...].astype(BF16), fold).astype(BF16)
+    slot = iota((256, 32), 0)
+    source = (slot // 16) * NLAT + lax.rem(slot, NLAT)
+    spread = mm(one_hot(source // 4 == iota((256, 32), 1)), counts)
+    slot = iota((256, 128), 0)
+    source = (slot // 16) * NLAT + lax.rem(slot, NLAT)
+    count = jnp.sum(
+        jnp.where(lax.rem(source, 4) == iota((256, 128), 1), spread, 0.0), axis=1, keepdims=True
+    )
     rank = (lax.rem(iota((256, CH), 0), 16) // NLAT).astype(F32)
-    live = jnp.where(mm(expand, counts) > rank + 0.5, 1.0, 0.0)
+    live = jnp.where(jnp.broadcast_to(count, (256, CH)) > rank + 0.5, 1.0, 0.0)
     live_ref[0:256] = live
     live_ref[256:512] = live
+    loads[4].wait()
     for a in range(7):
         for b in range(7):
             tap = kernels_ref[a, b].astype(F32)
@@ -581,6 +661,8 @@
     recv_b[block(lon)] = send_b[block(lon)]
     end_hop(along_lon, send_b, recv_b, 8, NLON)
 
+    loads[5].wait()
+    loads[6].wait()
     for token in range(2):
         tokens = recv_b[:, token * CH : token * CH + CH]
         rows = slice(token * 256, token * 256 + 256)
@@ -607,6 +689,8 @@
 
     loop(0, HEADS, attend)
 
+    for load in loads[7:]:
+        load.wait()
     state = (grid_ref[...].astype(F32) + mm_tn(ctx_t_ref[...], wo_ref[...])).astype(BF16)
     st_ref[0] = state.reshape(ROWS, COLS, CH)
 
@@ -614,6 +698,7 @@
         return Halo(
             place,
             tile,
+            halo_packed.at[index],
             halo_rows.at[index],
             halo_cols.at[index],
             halo_corners.at[index],
@@ -625,13 +710,12 @@
         edge.start()
         padded = pad_ref.at[layer]
         edge.fill_inner(padded)
-        edge.fill_edges(padded)
-
-        def store_mixed(half, chunk, sums):
-            for row in range(ROWS):
-                inner_ref[half, row, chunk * 16 : chunk * 16 + 16, :] = sums[row]
-
-        correlate(padded, taps_ref, layer, False, store_mixed)
+
+        correlate(padded, taps_ref, layer, False, True, inner_ref, (1, 2))
+        edge.fill_sides(padded)
+        correlate(padded, taps_ref, layer, False, True, inner_ref, (0, 3))
+        edge.fill_ends(padded)
+        correlate(padded, taps_ref, layer, False, False, inner_ref, range(4))
 
         def mix(row_pair):
             top = aligned(row_pair * 2, 2)
@@ -663,10 +747,14 @@
         loop(0, 4, mix)
 
     kgrad_ref[...] = jnp.zeros_like(kgrad_ref)
-    reduce_1 = Exchange(place, x_1, half_1, l1_1, part_1, l2_1, out_1, sems_1, BIG)
-    reduce_0 = Exchange(place, x_0, half_0, l1_0, part_0, l2_0, out_0, sems_0, BIG)
+    reduce_1 = Exchange(
+        place, True, False, x_1, half_1, l1_1, part_1, l2_1, out_1, sems_1, BIG
+    )
+    reduce_0 = Exchange(
+        place, False, False, x_0, half_0, l1_0, part_0, l2_0, out_0, sems_0, BIG
+    )
     reduce_att = Exchange(
-        place, x_attention, half_att, l1_att, part_att, l2_att, out_attention, sems_att, BIG
+        place, True, True, x_attention, half_att, l1_att, part_att, l2_att, out_attention, sems_att, BIG
     )
     reduce_k = SmallExchange(place, x_kernels, l1_k, part_k, l2_k, out_kernels, sems_k)
 
@@ -694,8 +782,6 @@
         loop(0, 4, unmix)
         edge = halo(2 + layer, gl_ref.at[layer])
         edge.start()
-        if layer == 0:
-            reduce_1.start_2()
         edge.fill_inner(pad_back)
 
         for piece in range(4):
@@ -707,32 +793,31 @@
         if layer == 1:
             reduce_1.start_0()
         else:
-            reduce_1.start_3()
             reduce_0.start_0()
+            reduce_1.start_2()
 
         for half in range(2):
             inner_ref[half] = pad_back[half, 3 : 3 + ROWS, 8 : 8 + COLS, :]
         kernel_grads(pad_ref.at[layer], inner_ref, kgrad_ref, layer)
-
-        edge.fill_edges(pad_back)
-
-        def add_direct(half, chunk, sums):
-            for row in range(ROWS):
-                inner_ref[half, row, chunk * 16 : chunk * 16 + 16, :] = sums[row]
-
-        correlate(pad_back, taps_ref, layer, True, add_direct)
+        if layer == 1:
+            reduce_1.start_1()
+        else:
+            reduce_0.start_1()
+
+        correlate(pad_back, taps_ref, layer, True, True, inner_ref, (1, 2))
+        edge.fill_sides(pad_back)
+        correlate(pad_back, taps_ref, layer, True, True, inner_ref, (0, 3))
+        edge.fill_ends(pad_back)
+        correlate(pad_back, taps_ref, layer, True, False, inner_ref, range(4))
         for half in range(2):
             lanes = slice(half * 128, half * 128 + 128)
             grad_ref[:, lanes] = grad_ref[:, lanes] + inner_ref[half].reshape(CELLS, 128)
-        if layer == 1:
-            reduce_1.start_1()
 
     x_kernels[0:112, 0:128] = kgrad_ref[0].astype(BF16)
     x_kernels[0:112, 128:256] = kgrad_ref[1].astype(BF16)
     x_kernels[112:128] = jnp.zeros((16, CH), BF16)
     reduce_k.start_0()
-    reduce_0.start_1()
-    reduce_1.start_4()
+    reduce_1.start_3()
 
     def put_attention(index, matrix):
         for half in range(2):
@@ -763,13 +848,12 @@
                 mm(kt_ref[head_rows(head), :], grad_scores) * SCALE
             ).astype(BF16)
 
-    loop(0, HEADS // 2, unattend)
-    reduce_1.start_5()
+    loop(0, 4, unattend)
+    reduce_k.start_1()
+    reduce_1.start_4()
     reduce_0.start_2()
-    reduce_k.start_1()
-    loop(HEADS // 2, HEADS, unattend)
+    loop(4, HEADS, unattend)
     reduce_0.start_3()
-    reduce_k.start_2()
 
     grad_keys = (dk_ref[...] * SCALE).astype(BF16)
     grad_values = dv_ref[...].astype(BF16)
@@ -788,6 +872,9 @@
             mm_tn(recv_b[:, :CH], grads[:256]) + mm_tn(recv_b[:, CH:], grads[256:]),
         )
     reduce_att.start_0()
+    reduce_k.start_2()
+    reduce_att.start_1()
+    reduce_1.start_5()
     reduce_0.start_4()
 
     end_hop(along_lon, back_b, got_b, 24, NLON)
@@ -797,17 +884,15 @@
         ).astype(BF16)
     start_hop(along_lat, back_a, got_a, 40, NLAT)
     got_a[block(lat)] = back_a[block(lat)]
-    reduce_att.start_1()
-    reduce_0.start_5()
-    reduce_k.finish()
+    reduce_att.start_2()
     end_hop(along_lat, back_a, got_a, 40, NLAT)
     grad_enc_ref[...] = mm_tn(chosen_ref[0], got_a[:, :512]) + mm_tn(chosen_ref[1], got_a[:, 512:])
-    reduce_att.start_2()
     reduce_1.finish()
+    reduce_k.finish()
     reduce_att.start_3()
+    reduce_0.start_5()
+    reduce_att.start_5()
     reduce_0.finish()
-    reduce_att.start_4()
-    reduce_att.start_5()
     reduce_att.finish()
 
 
@@ -823,7 +908,9 @@
     def sem(*shape):
         return pltpu.SemaphoreType.DMA(shape)
 
-    scratch = [
+    loaded = [pltpu.VMEM(operand.shape, operand.dtype) for operand in operands]
+    scratch = loaded + [
+        sem(len(operands)),
         b(2, DEVICES, BLOCKS_DEV),
         b(128, 1024),
         b(128, 1024),
@@ -834,6 +921,7 @@
         b(128, 1024),
         b(128, 1024),
         f(SLOTS, 256),
+        f(32, 384),
         b(CELLS, CH),
         b(CELLS, CH),
         b(CH, CELLS),
@@ -863,9 +951,10 @@
         b(CH, CELLS),
         f(SLOTS, CH),
         f(SLOTS, CH),
+        b(4, 2, 32, CH),
         b(4, 2, 3, COLS, CH),
-        b(4, 2, ROWS, 16, CH),
-        b(4, 4, 3, 16, CH),
+        b(4, 2, 32, CH),
+        b(4, 4, 16, CH),
         b(BIG, 128),
         b(KROWS, CH),
         b(BIG, CH),
@@ -879,7 +968,7 @@
         b(BIG // 16, 128),
         b(BIG // 16, CH),
         b(BIG // 16, CH),
-        b(NYZ, BIG // 128, 128),
+        b(NYZ, BIG // 16, 128),
         b(NYZ, BIG // 128, CH),
         b(NYZ, BIG // 128, CH),
         b(NLAT, 16, CH),
@@ -902,13 +991,69 @@
             jax.ShapeDtypeStruct((BIG, CH), BF16),
             jax.ShapeDtypeStruct((BIG, CH), BF16),
         ],
-        in_specs=[vm] * len(operands),
+        in_specs=[pl.BlockSpec(memory_space=pltpu.HBM)] * len(operands),
         out_specs=[vm] * 6,
         scratch_shapes=scratch,
         compiler_params=pltpu.CompilerParams(
             collective_id=0, has_side_effects=True, vmem_limit_bytes=56 * 1024 * 1024
         ),
         name="assimilate",
+    )(*operands)
+
+
+def finishing(
+    analysis_ref,
+    grad_enc_ref,
+    attention_ref,
+    taps_ref,
+    sums_1,
+    sums_0,
+    out_analysis,
+    out_enc,
+    out_attention,
+    out_taps,
+    out_expand,
+    out_reduce,
+    taps_f32,
+):
+    out_analysis[...] = analysis_ref[...]
+    for token in range(2):
+        out_enc[:, token, :] = grad_enc_ref[:, token * CH : token * CH + CH]
+    for index in range(4):
+        for half in range(2):
+            row = (index * 2 + half) * 256
+            out_attention[index, :, half * 128 : half * 128 + 128] = attention_ref[
+                row : row + 256
+            ].astype(F32)
+    taps_f32[...] = taps_ref[...].astype(F32)
+    for a in range(7):
+        for b in range(7):
+            row = (a * 7 + b) * 2
+            out_taps[a, b] = taps_f32[row : row + 2]
+    for layer, sums in enumerate((sums_0, sums_1)):
+        for piece in range(4):
+            rows = slice(piece * 256, piece * 256 + 256)
+            out_expand[layer, :, rows] = sums[rows].astype(F32)
+        out_reduce[layer] = sums[1024:].astype(F32)
+
+
+def finished(*operands):
+    vm = pl.BlockSpec(memory_space=pltpu.VMEM)
+    return pl.pallas_call(
+        finishing,
+        out_shape=[
+            jax.ShapeDtypeStruct((CELLS, CH), BF16),
+            jax.ShapeDtypeStruct((BLOCKS_DEV, 2, CH), F32),
+            jax.ShapeDtypeStruct((4, CH, CH), F32),
+            jax.ShapeDtypeStruct((7, 7, 2, CH), F32),
+            jax.ShapeDtypeStruct((2, CH, WIDE), F32),
+            jax.ShapeDtypeStruct((2, WIDE, CH), F32),
+        ],
+        in_specs=[vm] * 6,
+        out_specs=[vm] * 6,
+        scratch_shapes=[pltpu.VMEM((KROWS, CH), F32)],
+        compiler_params=pltpu.CompilerParams(vmem_limit_bytes=56 * 1024 * 1024),
+        name="finish",
     )(*operands)
 
 
@@ -925,10 +1070,10 @@
     w_reduce,
     cotangent,
 ):
-    analysis, grad_enc, attention, taps, sums_1, sums_0 = fused(
+    results = fused(
         grid_state.reshape(CELLS, CH),
-        encodings.reshape(BLOCKS_DEV, 2 * CH),
-        routes.T.reshape(2, DEVICES, BLOCKS_DEV),
+        encodings,
+        routes.T,
         w_query,
         w_key,
         w_value,
@@ -938,16 +1083,12 @@
         w_reduce,
         cotangent.reshape(CELLS, CH),
     )
-    attention = attention.astype(F32).reshape(4, 2, CH, 128).transpose(0, 2, 1, 3)
-    taps = taps[:112].astype(F32).reshape(2, 56, CH)[:, :49].reshape(2, 7, 7, CH)
-    both = jnp.stack([sums_0, sums_1]).astype(F32)
-    expand = both[:, :1024].reshape(2, 4, CH, CH).transpose(0, 2, 1, 3).reshape(2, CH, WIDE)
-    reduce = both[:, 1024:]
+    analysis, grad_enc, attention, taps, expand, reduce = finished(*results)
     return (
         analysis.reshape(ROWS, COLS, CH),
-        grad_enc.reshape(BLOCKS_DEV, 2, CH),
-        attention.reshape(4, CH, CH),
-        taps,
+        grad_enc,
+        attention,
+        taps.transpose(2, 0, 1, 3),
         expand,
         reduce,
     )

time: 164 us -> 133 us (0.81)
  Pallas kernels: 151 us -> 132 us
  local copies, waits for them, and re-layouts: 8.8 us -> 0 us
  other arithmetic: 2.88 us -> 0 us
    pallas_call x1, Pallas kernels: 151 us -> 127 us  [fused(): pl.pallas_call(kernel, out_shape=[jax.ShapeDtypeStruct((CELLS, CH), BF16)...]
    reshape x4 -> x0, local copies, waits for them, and re-layouts: 4.82 us -> none  [the longest x1 1.69 us: local(): routes.T.reshape(2, DEVICES, BLOCKS_DEV)]
    pallas_call x0 -> x1, Pallas kernels: none -> 4.56 us  [finished(): pl.pallas_call(finishing, out_shape=[jax.ShapeDtypeStruct((CELLS, CH), BF...]
    unnamed x10 -> x0, local copies, waits for them, and re-layouts: 2.26 us -> none
    convert_element_type x1 -> x0, other arithmetic: 1.81 us -> none  [local(): both = jnp.stack([sums_0, sums_1]).astype(F32)]
    slice x2 -> x0, local copies, waits for them, and re-layouts: 1.72 us -> none  [the longest x1 1.72 us: local(): reduce = both[:, 1024:]]
where the time goes in v1:
time: 133 us
  Pallas kernels  132 us (99%)
    pallas_call x1, Pallas kernels, fused(): pl.pallas_call(kernel, out_shape=[jax.ShapeDtypeStruct((CELLS, CH), BF16)...  127 us
    pallas_call x1, Pallas kernels, finished(): pl.pallas_call(finishing, out_shape=[jax.ShapeDtypeStruct((CELLS, CH), BF...  4.56 us

profile of v1, /device:TPU:1, one launch (start us, length us, event | category | flops | bytes accessed | tf_op | source)
XLA Modules:
  0.0 132.6 jit_solution(140388591764816349)
XLA Ops:
  0.6 127.4 %assimilate.1 = (bf16[512,256]{1,0:T(8,128)(2,1)}, f32[96,512]{1,0:T(8,128)}, bf16[2048,128]{1,0:T(8,128)(2,1)}, bf16[128,256]{1,0:T(8,128)(2,1)}, bf16[2048,256]{1,0:T(8,128)(2,1)}, /*index=5*/bf16[2048,256]{1,0:T(8,128)(2,1)}) custom-call(bf16[512,256]{1,0:T(8,128)(2,1)} %bitcast.6, bf16[96,2,256]{2,1,0:T(2,128)(2,1)} %enc_hbm.1, s32[2,12288]{1,0:T(2,128)} %bitcast.8, ...), custom_call_target="tpu_custom_call" | custom-call | tf_op jit(solution)/shard_map/assimilate/pallas_call | solution.py:984
  128.0 4.6 %finish.1 = (bf16[512,256]{1,0:T(8,128)(2,1)}, f32[96,2,256]{2,1,0:T(2,128)}, f32[4,256,256]{2,1,0:T(8,128)}, f32[7,7,2,256]{3,2,1,0:T(2,128)}, f32[2,256,1024]{2,1,0:T(8,128)}, /*index=5*/f32[2,1024,256]{2,1,0:T(8,128)}) custom-call(bf16[512,256]{1,0:T(8,128)(2,1)} %get-tuple-element.18.analysis_ref, f32[96,512]{1,0:T(8,128)} %get-tuple-element.19.grad_enc_ref, ...), custom_call_target="tpu_custom_call" | custom-call | tf_op jit(solution)/shard_map/finish/pallas_call | solution.py:1042

commit v2 on v1

--- a/solution.py
+++ b/solution.py
@@ -27,12 +27,13 @@
 SLOTS = 512
 EPSILON = 1e-06
 SCALE = 1.0 / math.sqrt(DEPTH)
+LOG2_E = math.log2(math.e)
 GELU_0 = math.sqrt(2.0 / math.pi)
 GELU_1 = GELU_0 * 0.044715
 PAD_ROWS = ROWS + 6
 PAD_COLS = 80
 BIG = 2048
-KROWS = 128
+ATT = BIG + 256
 
 
 def mm(a, b):
@@ -81,6 +82,10 @@
             device_id_type=MESH,
         )
 
+    def settle(self, phase, sent, arrived):
+        self.copy(sent, sent, phase, (self.lon, self.lat)).wait_send()
+        self.copy(arrived, arrived, phase, (self.lon, self.lat)).wait_recv()
+
     def pair(self):
         return (self.lon + 1 - 2 * self.core, self.lat)
 
@@ -113,7 +118,7 @@
         return self.copy(
             self.half.at[pl.ds(aligned(peer * self.r2, self.r2), self.r2)],
             self.level_1.at[k],
-            k,
+            1,
             self.device(self.lat_first, peer),
         )
 
@@ -136,16 +141,16 @@
         peer = self.to_second(k)
         device = self.device(not self.lat_first, peer)
         if self.whole:
-            return self.copy(self.part, self.level_2.at[k], 8 + k, device)
+            return self.copy(self.part, self.level_2.at[k], 2, device)
         return self.copy(
             self.part.at[pl.ds(aligned(peer * self.r3, self.r3), self.r3)],
             self.level_2.at[k],
-            8 + k,
+            2,
             device,
         )
 
     def start_2(self):
-        loop(1, 8, lambda k: self.copy_1(k).wait())
+        self.settle(1, self.half.at[pl.ds(0, 7 * self.r2)], self.level_1.at[pl.ds(1, 7)])
         total = self.half[pl.ds(aligned(self.first * self.r2, self.r2), self.r2)].astype(F32)
         for k in range(1, 8):
             total = total + self.level_1[k].astype(F32)
@@ -158,10 +163,11 @@
     def copy_3(self, k):
         rows = pl.ds(aligned(self.offset(self.first, self.second), self.r3), self.r3)
         device = self.device(not self.lat_first, self.to_second(k))
-        return self.copy(self.total.at[rows], self.total.at[rows], 16 + k, device)
+        return self.copy(self.total.at[rows], self.total.at[rows], 3, device)
 
     def start_3(self):
-        loop(1, 8, lambda k: self.copy_2(k).wait())
+        sent = self.half.at[pl.ds(0, 7 * self.r2)] if self.whole else self.part.at[pl.ds(0, 7 * self.r3)]
+        self.settle(2, sent, self.level_2.at[pl.ds(1, 7)])
         if self.whole:
             self.level_2[0] = self.part[...]
             total = jnp.zeros(self.part.shape, F32)
@@ -181,103 +187,25 @@
     def copy_4(self, k):
         rows = pl.ds(aligned(self.offset(self.first, 0), self.r2), self.r2)
         device = self.device(self.lat_first, self.to_first(k))
-        return self.copy(self.total.at[rows], self.total.at[rows], 24 + k, device)
+        return self.copy(self.total.at[rows], self.total.at[rows], 4, device)
 
     def start_4(self):
-        def settle(k):
-            self.copy_3(k).wait_send()
-            rows = pl.ds(aligned(self.offset(self.first, self.from_second(k)), self.r3), self.r3)
-            self.copy(
-                self.total.at[rows], self.total.at[rows], 16 + k, (self.lon, self.lat)
-            ).wait_recv()
-
-        loop(1, 8, settle)
+        rows = self.total.at[pl.ds(0, 7 * self.r3)]
+        self.settle(3, rows, rows)
         loop(1, 8, lambda k: self.copy_4(k).start())
 
     def copy_5(self):
         rows = pl.ds(aligned(self.core * self.r1, self.r1), self.r1)
-        return self.copy(self.total.at[rows], self.total.at[rows], 8, self.pair())
+        return self.copy(self.total.at[rows], self.total.at[rows], 5, self.pair())
 
     def start_5(self):
-        def settle(k):
-            self.copy_4(k).wait_send()
-            rows = pl.ds(aligned(self.offset(self.from_first(k), 0), self.r2), self.r2)
-            self.copy(
-                self.total.at[rows], self.total.at[rows], 24 + k, (self.lon, self.lat)
-            ).wait_recv()
-
-        loop(1, 8, settle)
+        rows = self.total.at[pl.ds(0, 7 * self.r2)]
+        self.settle(4, rows, rows)
         self.copy_5().start()
 
     def finish(self):
-        self.copy_5().wait_send()
-        rows = pl.ds(aligned((1 - self.core) * self.r1, self.r1), self.r1)
-        self.copy(
-            self.total.at[rows], self.total.at[rows], 8, (self.lon, self.lat)
-        ).wait_recv()
-
-
-class SmallExchange:
-    def __init__(self, place, source, level_1, part, level_2, total, sems):
-        self.lon, self.lat, self.core, self.yz = place
-        self.source, self.level_1, self.part = source, level_1, part
-        self.level_2, self.total, self.sems = level_2, total, sems
-
-    def copy(self, src, dst, index, lon, lat):
-        return pltpu.make_async_remote_copy(
-            src_ref=src,
-            dst_ref=dst,
-            send_sem=self.sems.at[0, index],
-            recv_sem=self.sems.at[1, index],
-            device_id=(lon, lat),
-            device_id_type=MESH,
-        )
-
-    def copy_0(self, k):
-        peer = lax.rem(self.lat + k, NLAT)
-        return self.copy(
-            self.source.at[pl.ds(aligned(peer * 16, 16), 16)], self.level_1.at[k], k, self.lon, peer
-        )
-
-    def start_0(self):
-        loop(1, NLAT, lambda k: self.copy_0(k).start())
-
-    def copy_1(self, k):
-        peer = lax.rem(self.lon + k, NLON)
-        return self.copy(self.part.at[...], self.level_2.at[k], 8 + k, peer, self.lat)
-
-    def start_1(self):
-        loop(1, NLAT, lambda k: self.copy_0(k).wait())
-        total = self.source[pl.ds(aligned(self.lat * 16, 16), 16)].astype(F32)
-        for k in range(1, NLAT):
-            total = total + self.level_1[k].astype(F32)
-        self.part[...] = total.astype(BF16)
-        loop(1, NLON, lambda k: self.copy_1(k).start())
-
-    def copy_2(self, k):
-        rows = pl.ds(aligned(self.lat * 16, 16), 16)
-        peer = lax.rem(self.lat + k, NLAT)
-        return self.copy(self.total.at[rows], self.total.at[rows], 24 + k, self.lon, peer)
-
-    def start_2(self):
-        loop(1, NLON, lambda k: self.copy_1(k).wait())
-        self.level_2[0] = self.part[...]
-        total = jnp.zeros((16, CH), F32)
-        for index in range(NLON):
-            slot = lax.rem(self.lon - index + NLON, NLON)
-            total = total + self.level_2[slot].astype(F32)
-        self.total[pl.ds(aligned(self.lat * 16, 16), 16)] = total.astype(BF16)
-        loop(1, NLAT, lambda k: self.copy_2(k).start())
-
-    def finish(self):
-        def settle(k):
-            self.copy_2(k).wait_send()
-            rows = pl.ds(aligned(lax.rem(self.lat + NLAT - k, NLAT) * 16, 16), 16)
-            self.copy(
-                self.total.at[rows], self.total.at[rows], 24 + k, self.lon, self.lat
-            ).wait_recv()
-
-        loop(1, NLAT, settle)
+        rows = self.total.at[pl.ds(0, self.r1)]
+        self.settle(5, rows, rows)
 
 
 class Halo:
@@ -304,14 +232,27 @@
             pltpu.make_async_remote_copy(
                 src_ref=src,
                 dst_ref=dst,
-                send_sem=self.sems.at[0, index],
-                recv_sem=self.sems.at[1, index],
+                send_sem=self.sems.at[0, (0, 0, 1, 1, 2, 2, 2, 2)[index]],
+                recv_sem=self.sems.at[1, (0, 0, 1, 1, 2, 2, 2, 2)[index]],
                 device_id=(lon, lat),
                 device_id_type=MESH,
             )
             for index, (src, dst, lon, lat) in enumerate(plan)
             if index in wanted
         ]
+
+    def settle(self, kind):
+        buffer = (self.rows, self.cols, self.corners)[kind]
+        copy = pltpu.make_async_remote_copy(
+            src_ref=buffer,
+            dst_ref=buffer,
+            send_sem=self.sems.at[0, kind],
+            recv_sem=self.sems.at[1, kind],
+            device_id=(self.lon, self.lat),
+            device_id_type=MESH,
+        )
+        copy.wait_send()
+        copy.wait_recv()
 
     def start(self):
         for copy in self.copies((0, 1)):
@@ -330,8 +271,7 @@
                 padded[half, 3 + row, 8 : 8 + COLS, :] = cells[:, half * 128 : half * 128 + 128]
 
     def fill_sides(self, padded):
-        for copy in self.copies((2, 3)):
-            copy.wait()
+        self.settle(1)
         for side, col in ((0, 4), (1, 8 + COLS)):
             cells = self.cols[side].astype(F32)
             for row in range(ROWS):
@@ -341,8 +281,8 @@
                     ]
 
     def fill_ends(self, padded):
-        for copy in self.copies((0, 1, 4, 5, 6, 7)):
-            copy.wait()
+        self.settle(0)
+        self.settle(2)
         has_north = jnp.where(self.lat > 0, 1.0, 0.0).astype(F32)
         has_south = jnp.where(self.lat < NLAT - 1, 1.0, 0.0).astype(F32)
         for end, there, start, skip in ((0, has_north, 0, 1), (1, has_south, 3 + ROWS, 0)):
@@ -433,12 +373,11 @@
     we_hbm,
     wr_hbm,
     cot_hbm,
-    analysis_ref,
-    grad_enc_ref,
-    out_attention,
-    out_kernels,
-    out_1,
-    out_0,
+    analysis_hbm,
+    grad_enc_hbm,
+    attention_hbm,
+    sums_1_hbm,
+    sums_0_hbm,
     grid_ref,
     enc_ref,
     routes_ref,
@@ -451,6 +390,12 @@
     wr_ref,
     cot_ref,
     load_sems,
+    analysis_ref,
+    grad_enc_ref,
+    out_attention,
+    out_1,
+    out_0,
+    store_sems,
     chosen_ref,
     send_a,
     recv_a,
@@ -460,11 +405,11 @@
     got_b,
     back_a,
     got_a,
-    live_ref,
+    dead_ref,
     group_ref,
     normed_ref,
-    q_ref,
     qt_ref,
+    qt_one_ref,
     k_ref,
     kt_ref,
     v_ref,
@@ -486,17 +431,16 @@
     gpre_ref,
     grad_ref,
     low_ref,
-    gctx_ref,
     gt_ref,
     dq_t_ref,
-    dk_ref,
-    dv_ref,
+    dk_t_ref,
+    dv_t_ref,
+    scores_ref,
     halo_packed,
     halo_rows,
     halo_cols,
     halo_corners,
     x_attention,
-    x_kernels,
     x_1,
     x_0,
     half_att,
@@ -511,15 +455,11 @@
     l2_att,
     l2_1,
     l2_0,
-    l1_k,
-    part_k,
-    l2_k,
     a2a_sems,
     halo_sems,
     sems_att,
     sems_1,
     sems_0,
-    sems_k,
 ):
     lon, lat = lax.axis_index("lon"), lax.axis_index("lat")
     core, yz = lax.rem(lon, 2), lon // 2
@@ -545,6 +485,17 @@
     ]
     for load in loads:
         load.start()
+    results = (
+        (analysis_ref, analysis_hbm),
+        (grad_enc_ref, grad_enc_hbm),
+        (out_attention, attention_hbm),
+        (out_1, sums_1_hbm),
+        (out_0, sums_0_hbm),
+    )
+    stores = [
+        pltpu.make_async_copy(source, target, store_sems.at[index])
+        for index, (source, target) in enumerate(results)
+    ]
 
     barrier = pltpu.get_barrier_semaphore()
 
@@ -593,27 +544,21 @@
     def block(index):
         return pl.ds(aligned(index * 16, 16), 16)
 
-    def along_lat(src, dst, base, k, incoming):
-        peer = lax.rem(lat + (NLAT - k if incoming else k), NLAT)
-        if incoming:
-            return a2a(src.at[block(peer)], dst.at[block(peer)], base + k, lon, lat)
-        return a2a(src.at[block(peer)], dst.at[block(lat)], base + k, lon, peer)
-
-    def along_lon(src, dst, base, k, incoming):
-        peer = lax.rem(lon + (NLON - k if incoming else k), NLON)
-        if incoming:
-            return a2a(src.at[block(peer)], dst.at[block(peer)], base + k, lon, lat)
-        return a2a(src.at[block(peer)], dst.at[block(lon)], base + k, peer, lat)
-
-    def start_hop(route, src, dst, base, count):
-        loop(1, count, lambda k: route(src, dst, base, k, False).start())
-
-    def end_hop(route, src, dst, base, count):
-        def settle(k):
-            route(src, dst, base, k, False).wait_send()
-            route(src, dst, base, k, True).wait_recv()
-
-        loop(1, count, settle)
+    def along_lat(src, dst, hop, k):
+        peer = lax.rem(lat + k, NLAT)
+        return a2a(src.at[block(peer)], dst.at[block(lat)], hop, lon, peer)
+
+    def along_lon(src, dst, hop, k):
+        peer = lax.rem(lon + k, NLON)
+        return a2a(src.at[block(peer)], dst.at[block(lon)], hop, peer, lat)
+
+    def start_hop(route, src, dst, hop, count):
+        loop(1, count, lambda k: route(src, dst, hop, k).start())
+
+    def end_hop(src, dst, hop, count):
+        rows = pl.ds(0, (count - 1) * 16)
+        a2a(src.at[rows], src.at[rows], hop, lon, lat).wait_send()
+        a2a(dst.at[rows], dst.at[rows], hop, lon, lat).wait_recv()
 
     start_hop(along_lat, send_a, recv_a, 0, NLAT)
     recv_a[block(lat)] = send_a[block(lat)]
@@ -623,8 +568,15 @@
     normed = normalise(grid_ref[...].astype(F32))[0].astype(BF16)
     normed_ref[...] = normed
     queries = mm(normed, wq_ref[...]).astype(BF16)
-    q_ref[...] = queries
-    qt_ref[...] = queries.T
+    queries_t = queries.T
+    qt_ref[...] = queries_t
+    for odd in range(2):
+        row = DEPTH * (1 - odd)
+        qt_one_ref[odd] = queries_t
+        first = queries_t[row : row + 16].astype(F32)
+        qt_one_ref[odd, row : row + 16, :] = jnp.where(iota((16, CELLS), 0) == 0, 1.0, first).astype(
+            BF16
+        )
     mine = jnp.sum(jnp.where(routes_ref[...] == me, 1.0, 0.0), axis=0, keepdims=True)
     for group in range(32):
         group_ref[group : group + 1, :] = mine[:, group * 384 : group * 384 + 384]
@@ -639,9 +591,13 @@
         jnp.where(lax.rem(source, 4) == iota((256, 128), 1), spread, 0.0), axis=1, keepdims=True
     )
     rank = (lax.rem(iota((256, CH), 0), 16) // NLAT).astype(F32)
-    live = jnp.where(jnp.broadcast_to(count, (256, CH)) > rank + 0.5, 1.0, 0.0)
-    live_ref[0:256] = live
-    live_ref[256:512] = live
+    for odd in range(2):
+        silent = (jnp.broadcast_to(count, (256, CH)) < rank + 0.5) & (
+            iota((256, CH), 1) == DEPTH * (1 - odd)
+        )
+        dead = jnp.where(silent, -1e30, 0.0).astype(BF16)
+        dead_ref[odd, 0:256] = dead
+        dead_ref[odd, 256:512] = dead
     loads[4].wait()
     for a in range(7):
         for b in range(7):
@@ -653,13 +609,13 @@
     shuffle = one_hot(
         (lax.rem(out_row, 16) // NLAT) * 128 + lax.rem(out_row, NLAT) * 16 + out_row // 16 == in_row
     )
-    end_hop(along_lat, send_a, recv_a, 0, NLAT)
+    end_hop(send_a, recv_a, 0, NLAT)
     send_b[...] = (
         mm(shuffle[:, :128], recv_a[:, :512]) + mm(shuffle[:, 128:], recv_a[:, 512:])
     ).astype(BF16)
-    start_hop(along_lon, send_b, recv_b, 8, NLON)
+    start_hop(along_lon, send_b, recv_b, 1, NLON)
     recv_b[block(lon)] = send_b[block(lon)]
-    end_hop(along_lon, send_b, recv_b, 8, NLON)
+    end_hop(send_b, recv_b, 1, NLON)
 
     loads[5].wait()
     loads[6].wait()
@@ -677,17 +633,21 @@
     def head_rows(head):
         return pl.ds(aligned(head * DEPTH, DEPTH), DEPTH)
 
-    def attend(head):
-        keys = k_ref[...] * head_mask(head)
-        for part in range(2):
-            cells = slice(part * 256, part * 256 + 256)
-            raised = jnp.exp(mm(keys, qt_ref[:, cells]) * SCALE) * live_ref[...]
-            weights = raised * (1.0 / jnp.sum(raised, axis=0, keepdims=True))
-            probs = weights.astype(BF16)
-            probs_ref[head, :, cells] = probs
-            ctx_t_ref[head_rows(head), cells] = mm(vt_ref[head_rows(head), :], probs).astype(BF16)
-
-    loop(0, HEADS, attend)
+    def attend(head_pair):
+        for odd in range(2):
+            head = head_pair * 2 + odd
+            keys = k_ref[...] * head_mask(head) + dead_ref[odd]
+            for part in range(2):
+                cells = slice(part * 256, part * 256 + 256)
+                raised = jnp.exp2(mm(keys, qt_one_ref[odd, :, cells]) * (SCALE * LOG2_E))
+                weights = raised * (1.0 / jnp.sum(raised, axis=0, keepdims=True))
+                probs = weights.astype(BF16)
+                probs_ref[head, :, cells] = probs
+                ctx_t_ref[head_rows(head), cells] = mm(vt_ref[head_rows(head), :], probs).astype(
+                    BF16
+                )
+
+    loop(0, HEADS // 2, attend)
 
     for load in loads[7:]:
         load.wait()
@@ -747,6 +707,7 @@
         loop(0, 4, mix)
 
     kgrad_ref[...] = jnp.zeros_like(kgrad_ref)
+    stores[0].start()
     reduce_1 = Exchange(
         place, True, False, x_1, half_1, l1_1, part_1, l2_1, out_1, sems_1, BIG
     )
@@ -754,9 +715,8 @@
         place, False, False, x_0, half_0, l1_0, part_0, l2_0, out_0, sems_0, BIG
     )
     reduce_att = Exchange(
-        place, True, True, x_attention, half_att, l1_att, part_att, l2_att, out_attention, sems_att, BIG
+        place, True, True, x_attention, half_att, l1_att, part_att, l2_att, out_attention, sems_att, ATT
     )
-    reduce_k = SmallExchange(place, x_kernels, l1_k, part_k, l2_k, out_kernels, sems_k)
 
     grad_ref[...] = cot_ref[...].astype(F32)
     for layer in (1, 0):
@@ -813,10 +773,10 @@
             lanes = slice(half * 128, half * 128 + 128)
             grad_ref[:, lanes] = grad_ref[:, lanes] + inner_ref[half].reshape(CELLS, 128)
 
-    x_kernels[0:112, 0:128] = kgrad_ref[0].astype(BF16)
-    x_kernels[0:112, 128:256] = kgrad_ref[1].astype(BF16)
-    x_kernels[112:128] = jnp.zeros((16, CH), BF16)
-    reduce_k.start_0()
+    for half in range(2):
+        row = BIG + half * 128
+        x_attention[row : row + 112] = kgrad_ref[half].astype(BF16)
+        x_attention[row + 112 : row + 128] = jnp.zeros((16, 128), BF16)
     reduce_1.start_3()
 
     def put_attention(index, matrix):
@@ -827,78 +787,74 @@
     low = grad_ref[...].astype(BF16)
     put_attention(3, mm(ctx_t_ref[...], low))
     gctx = mm_nt(low, wo_ref[...]).astype(BF16)
-    gctx_ref[...] = gctx
     gt_ref[...] = gctx.T
-    dk_ref[...] = jnp.zeros_like(dk_ref)
-    dv_ref[...] = jnp.zeros_like(dv_ref)
-
-    def unattend(head):
-        mask = head_mask(head)
-        values = v_ref[...] * mask
-        for part in range(2):
-            cells = slice(part * 256, part * 256 + 256)
-            probs = probs_ref[head, :, cells]
-            weights = probs.astype(F32)
-            grad_probs = mm(values, gt_ref[:, cells])
-            mean = jnp.sum(weights * grad_probs, axis=0, keepdims=True)
-            grad_scores = (weights * (grad_probs - mean)).astype(BF16)
-            dv_ref[...] += mm(probs, gctx_ref[cells] * mask)
-            dk_ref[...] += mm(grad_scores, q_ref[cells] * mask)
-            dq_t_ref[head_rows(head), cells] = (
-                mm(kt_ref[head_rows(head), :], grad_scores) * SCALE
-            ).astype(BF16)
-
-    loop(0, 4, unattend)
-    reduce_k.start_1()
+
+    def unattend(head_pair):
+        for odd in range(2):
+            head = head_pair * 2 + odd
+            mine = head_rows(head)
+            values = v_ref[...] * head_mask(head)
+            for part in range(2):
+                cells = slice(part * 256, part * 256 + 256)
+                weights = probs_ref[head, :, cells].astype(F32)
+                grad_probs = mm(values, gt_ref[:, cells])
+                mean = jnp.sum(weights * grad_probs, axis=0, keepdims=True)
+                scores_ref[odd, :, cells] = (weights * (grad_probs - mean)).astype(BF16)
+            dv_t_ref[mine, :] = mm_nt(gt_ref[mine, :], probs_ref[head]).astype(BF16)
+            grad_scores = scores_ref[odd]
+            dk_t_ref[mine, :] = (mm_nt(qt_ref[mine, :], grad_scores) * SCALE).astype(BF16)
+            dq_t_ref[mine, :] = (mm(kt_ref[mine, :], grad_scores) * SCALE).astype(BF16)
+
+    loop(0, 2, unattend)
     reduce_1.start_4()
     reduce_0.start_2()
-    loop(4, HEADS, unattend)
+    loop(2, 4, unattend)
     reduce_0.start_3()
 
-    grad_keys = (dk_ref[...] * SCALE).astype(BF16)
-    grad_values = dv_ref[...].astype(BF16)
+    grad_keys = dk_t_ref[...].T
+    grad_values = dv_t_ref[...].T
     for token in range(2):
         rows = slice(token * 256, token * 256 + 256)
         back_b[:, token * CH : token * CH + CH] = (
             mm_nt(grad_keys[rows], wk_ref[...]) + mm_nt(grad_values[rows], wv_ref[...])
         ).astype(BF16)
-    start_hop(along_lon, back_b, got_b, 24, NLON)
+    start_hop(along_lon, back_b, got_b, 2, NLON)
     got_b[block(lon)] = back_b[block(lon)]
 
-    put_attention(0, mm(dq_t_ref[...], normed_ref[...]).T)
-    for index, grads in ((1, grad_keys), (2, grad_values)):
-        put_attention(
-            index,
-            mm_tn(recv_b[:, :CH], grads[:256]) + mm_tn(recv_b[:, CH:], grads[256:]),
-        )
+    put_attention(0, mm(dq_t_ref[...], normed_ref[...]).astype(BF16).T)
+    for index, grads in ((1, dk_t_ref), (2, dv_t_ref)):
+        sums = mm(grads[:, :256], recv_b[:, :CH]) + mm(grads[:, 256:], recv_b[:, CH:])
+        put_attention(index, sums.astype(BF16).T)
     reduce_att.start_0()
-    reduce_k.start_2()
     reduce_att.start_1()
     reduce_1.start_5()
     reduce_0.start_4()
 
-    end_hop(along_lon, back_b, got_b, 24, NLON)
+    end_hop(back_b, got_b, 2, NLON)
     for c in range(2):
         back_a[:, c * 512 : c * 512 + 512] = mm_tn(
             shuffle[:, c * 128 : c * 128 + 128], got_b[...]
         ).astype(BF16)
-    start_hop(along_lat, back_a, got_a, 40, NLAT)
+    start_hop(along_lat, back_a, got_a, 3, NLAT)
     got_a[block(lat)] = back_a[block(lat)]
     reduce_att.start_2()
-    end_hop(along_lat, back_a, got_a, 40, NLAT)
+    end_hop(back_a, got_a, 3, NLAT)
     grad_enc_ref[...] = mm_tn(chosen_ref[0], got_a[:, :512]) + mm_tn(chosen_ref[1], got_a[:, 512:])
+    stores[1].start()
     reduce_1.finish()
-    reduce_k.finish()
+    stores[3].start()
     reduce_att.start_3()
     reduce_0.start_5()
     reduce_att.start_5()
     reduce_0.finish()
+    stores[4].start()
     reduce_att.finish()
+    stores[2].start()
+    for store in stores:
+        store.wait()
 
 
 def fused(*operands):
-    vm = pl.BlockSpec(memory_space=pltpu.VMEM)
-
     def b(*shape):
         return pltpu.VMEM(shape, BF16)
 
@@ -909,8 +865,17 @@
         return pltpu.SemaphoreType.DMA(shape)
 
     loaded = [pltpu.VMEM(operand.shape, operand.dtype) for operand in operands]
+    results = [
+        jax.ShapeDtypeStruct((CELLS, CH), BF16),
+        jax.ShapeDtypeStruct((BLOCKS_DEV, 512), F32),
+        jax.ShapeDtypeStruct((ATT, 128), BF16),
+        jax.ShapeDtypeStruct((BIG, CH), BF16),
+        jax.ShapeDtypeStruct((BIG, CH), BF16),
+    ]
     scratch = loaded + [
         sem(len(operands)),
+        *[pltpu.VMEM(result.shape, result.dtype) for result in results],
+        sem(len(results)),
         b(2, DEVICES, BLOCKS_DEV),
         b(128, 1024),
         b(128, 1024),
@@ -920,11 +885,11 @@
         b(256, 512),
         b(128, 1024),
         b(128, 1024),
-        f(SLOTS, 256),
+        b(2, SLOTS, CH),
         f(32, 384),
         b(CELLS, CH),
-        b(CELLS, CH),
         b(CH, CELLS),
+        b(2, CH, CELLS),
         b(SLOTS, CH),
         b(CH, SLOTS),
         b(SLOTS, CH),
@@ -946,53 +911,41 @@
         b(CELLS, WIDE),
         f(CELLS, CH),
         b(CELLS, CH),
-        b(CELLS, CH),
         b(CH, CELLS),
         b(CH, CELLS),
-        f(SLOTS, CH),
-        f(SLOTS, CH),
+        b(CH, SLOTS),
+        b(CH, SLOTS),
+        b(2, SLOTS, CELLS),
         b(4, 2, 32, CH),
         b(4, 2, 3, COLS, CH),
         b(4, 2, 32, CH),
         b(4, 4, 16, CH),
-        b(BIG, 128),
-        b(KROWS, CH),
+        b(ATT, 128),
         b(BIG, CH),
         b(BIG, CH),
-        b(BIG // 2, 128),
+        b(ATT // 2, 128),
         b(BIG // 2, CH),
         b(BIG // 2, CH),
-        b(NLAT, BIG // 16, 128),
+        b(NLAT, ATT // 16, 128),
         b(NLAT, BIG // 16, CH),
         b(NLAT, BIG // 16, CH),
-        b(BIG // 16, 128),
+        b(ATT // 16, 128),
         b(BIG // 16, CH),
         b(BIG // 16, CH),
-        b(NYZ, BIG // 16, 128),
+        b(NYZ, ATT // 16, 128),
         b(NYZ, BIG // 128, CH),
         b(NYZ, BIG // 128, CH),
-        b(NLAT, 16, CH),
-        b(16, CH),
-        b(NLON, 16, CH),
-        sem(2, 48),
-        sem(4, 2, 8),
-        sem(2, 32),
-        sem(2, 32),
-        sem(2, 32),
-        sem(2, 32),
+        sem(2, 4),
+        sem(4, 2, 3),
+        sem(2, 6),
+        sem(2, 6),
+        sem(2, 6),
     ]
     return pl.pallas_call(
         kernel,
-        out_shape=[
-            jax.ShapeDtypeStruct((CELLS, CH), BF16),
-            jax.ShapeDtypeStruct((BLOCKS_DEV, 512), F32),
-            jax.ShapeDtypeStruct((BIG, 128), BF16),
-            jax.ShapeDtypeStruct((KROWS, CH), BF16),
-            jax.ShapeDtypeStruct((BIG, CH), BF16),
-            jax.ShapeDtypeStruct((BIG, CH), BF16),
-        ],
+        out_shape=results,
         in_specs=[pl.BlockSpec(memory_space=pltpu.HBM)] * len(operands),
-        out_specs=[vm] * 6,
+        out_specs=[pl.BlockSpec(memory_space=pltpu.HBM)] * 5,
         scratch_shapes=scratch,
         compiler_params=pltpu.CompilerParams(
             collective_id=0, has_side_effects=True, vmem_limit_bytes=56 * 1024 * 1024
@@ -1002,43 +955,97 @@
 
 
 def finishing(
-    analysis_ref,
-    grad_enc_ref,
-    attention_ref,
-    taps_ref,
-    sums_1,
-    sums_0,
+    analysis_hbm,
+    grad_enc_hbm,
+    attention_hbm,
+    sums_1_hbm,
+    sums_0_hbm,
     out_analysis,
     out_enc,
     out_attention,
     out_taps,
     out_expand,
     out_reduce,
+    sums_in,
+    attention_in,
+    analysis_in,
+    enc_in,
+    expand,
+    reduce,
+    attention,
+    taps,
     taps_f32,
+    enc,
+    in_sems,
+    out_sems,
 ):
-    out_analysis[...] = analysis_ref[...]
-    for token in range(2):
-        out_enc[:, token, :] = grad_enc_ref[:, token * CH : token * CH + CH]
+    expand_rows, reduce_rows = pl.ds(0, WIDE), pl.ds(WIDE, WIDE)
+    inward = (
+        (sums_0_hbm.at[expand_rows], sums_in.at[0, expand_rows]),
+        (sums_0_hbm.at[reduce_rows], sums_in.at[0, reduce_rows]),
+        (sums_1_hbm.at[expand_rows], sums_in.at[1, expand_rows]),
+        (sums_1_hbm.at[reduce_rows], sums_in.at[1, reduce_rows]),
+        (attention_hbm, attention_in),
+        (grad_enc_hbm, enc_in),
+        (analysis_hbm, analysis_in),
+    )
+    outward = (
+        (expand.at[0], out_expand.at[0]),
+        (reduce.at[0], out_reduce.at[0]),
+        (expand.at[1], out_expand.at[1]),
+        (reduce.at[1], out_reduce.at[1]),
+        (attention, out_attention),
+        (taps, out_taps),
+        (enc, out_enc),
+        (analysis_in, out_analysis),
+    )
+    loads = [
+        pltpu.make_async_copy(source, target, in_sems.at[index])
+        for index, (source, target) in enumerate(inward)
+    ]
+    stores = [
+        pltpu.make_async_copy(source, target, out_sems.at[index])
+        for index, (source, target) in enumerate(outward)
+    ]
+    for load in loads:
+        load.start()
+    for layer in range(2):
+        loads[2 * layer].wait()
+        for piece in range(4):
+            rows = slice(piece * 256, piece * 256 + 256)
+            expand[layer, :, rows] = sums_in[layer, rows].astype(F32)
+        stores[2 * layer].start()
+        loads[2 * layer + 1].wait()
+        reduce[layer] = sums_in[layer, WIDE:].astype(F32)
+        stores[2 * layer + 1].start()
+    loads[4].wait()
     for index in range(4):
         for half in range(2):
             row = (index * 2 + half) * 256
-            out_attention[index, :, half * 128 : half * 128 + 128] = attention_ref[
+            attention[index, :, half * 128 : half * 128 + 128] = attention_in[
                 row : row + 256
             ].astype(F32)
-    taps_f32[...] = taps_ref[...].astype(F32)
+    stores[4].start()
+    for half in range(2):
+        row = BIG + half * 128
+        taps_f32[:, half * 128 : half * 128 + 128] = attention_in[row : row + 128].astype(F32)
     for a in range(7):
         for b in range(7):
             row = (a * 7 + b) * 2
-            out_taps[a, b] = taps_f32[row : row + 2]
-    for layer, sums in enumerate((sums_0, sums_1)):
-        for piece in range(4):
-            rows = slice(piece * 256, piece * 256 + 256)
-            out_expand[layer, :, rows] = sums[rows].astype(F32)
-        out_reduce[layer] = sums[1024:].astype(F32)
+            taps[a, b] = taps_f32[row : row + 2]
+    stores[5].start()
+    loads[6].wait()
+    stores[7].start()
+    loads[5].wait()
+    for token in range(2):
+        enc[:, token, :] = enc_in[:, token * CH : token * CH + CH]
+    stores[6].start()
+    for store in stores:
+        store.wait()
 
 
 def finished(*operands):
-    vm = pl.BlockSpec(memory_space=pltpu.VMEM)
+    hbm = pl.BlockSpec(memory_space=pltpu.HBM)
     return pl.pallas_call(
         finishing,
         out_shape=[
@@ -1049,9 +1056,22 @@
             jax.ShapeDtypeStruct((2, CH, WIDE), F32),
             jax.ShapeDtypeStruct((2, WIDE, CH), F32),
         ],
-        in_specs=[vm] * 6,
-        out_specs=[vm] * 6,
-        scratch_shapes=[pltpu.VMEM((KROWS, CH), F32)],
+        in_specs=[hbm] * 5,
+        out_specs=[hbm] * 6,
+        scratch_shapes=[
+            pltpu.VMEM((2, BIG, CH), BF16),
+            pltpu.VMEM((ATT, 128), BF16),
+            pltpu.VMEM((CELLS, CH), BF16),
+            pltpu.VMEM((BLOCKS_DEV, 512), F32),
+            pltpu.VMEM((2, CH, WIDE), F32),
+            pltpu.VMEM((2, WIDE, CH), F32),
+            pltpu.VMEM((4, CH, CH), F32),
+            pltpu.VMEM((7, 7, 2, CH), F32),
+            pltpu.VMEM((128, CH), F32),
+            pltpu.VMEM((BLOCKS_DEV, 2, CH), F32),
+            pltpu.SemaphoreType.DMA((7,)),
+            pltpu.SemaphoreType.DMA((8,)),
+        ],
         compiler_params=pltpu.CompilerParams(vmem_limit_bytes=56 * 1024 * 1024),
         name="finish",
     )(*operands)

time: 133 us -> 128 us (0.962)
  Pallas kernels: 132 us -> 127 us
    pallas_call x1, Pallas kernels: 127 us -> 124 us  [fused(): pl.pallas_call(kernel, out_shape=results, in_specs=[pl.BlockSpec(memory_s...]
where the time goes in v2:
time: 128 us
  Pallas kernels  127 us (99%)
    pallas_call x1, Pallas kernels, fused(): pl.pallas_call(kernel, out_shape=results, in_specs=[pl.BlockSpec(memory_s...  124 us
    pallas_call x1, Pallas kernels, finished(): pl.pallas_call(finishing, out_shape=[jax.ShapeDtypeStruct((CELLS, CH), BF...  3.73 us

profile of v2, /device:TPU:1, one launch (start us, length us, event | category | flops | bytes accessed | tf_op | source)
XLA Modules:
  0.0 128.1 jit_solution(17513029001744086288)
XLA Ops:
  0.6 123.6 %assimilate.1 = (bf16[512,256]{1,0:T(8,128)(2,1)}, f32[96,512]{1,0:T(8,128)}, bf16[2304,128]{1,0:T(8,128)(2,1)}, bf16[2048,256]{1,0:T(8,128)(2,1)}, bf16[2048,256]{1,0:T(8,128)(2,1)}) custom-call(bf16[512,256]{1,0:T(8,128)(2,1)} %bitcast.6, bf16[96,2,256]{2,1,0:T(2,128)(2,1)} %enc_hbm.1, s32[2,12288]{1,0:T(2,128)} %bitcast.8, bf16[256,256]{1,0:T(8,128)(2,1)} %wq_hbm.1, ...), custom_call_target="tpu_custom_call" | custom-call | tf_op jit(solution)/shard_map/assimilate/pallas_call | solution.py:944
  124.2 3.7 %finish.1 = (bf16[512,256]{1,0:T(8,128)(2,1)}, f32[96,2,256]{2,1,0:T(2,128)}, f32[4,256,256]{2,1,0:T(8,128)}, f32[7,7,2,256]{3,2,1,0:T(2,128)}, f32[2,256,1024]{2,1,0:T(8,128)}, /*index=5*/f32[2,1024,256]{2,1,0:T(8,128)}) custom-call(bf16[512,256]{1,0:T(8,128)(2,1)} %get-tuple-element.17.analysis_hbm, f32[96,512]{1,0:T(8,128)} %get-tuple-element.18.grad_enc_hbm, ...), custom_call_target="tpu_custom_call" | custom-call | tf_op jit(solution)/shard_map/finish/pallas_call | solution.py:1049

commit v3 on v2

--- a/solution.py
+++ b/solution.py
@@ -352,6 +352,14 @@
 
 def one_hot(condition):
     return jnp.where(condition, 1.0, 0.0).astype(BF16)
+
+
+def gelu(values):
+    square = values * values
+    curve = jnp.tanh(values * (GELU_0 + GELU_1 * square))
+    gate = 0.5 + 0.5 * curve
+    slope = gate + 0.5 * values * (1.0 - curve * curve) * (GELU_0 + 3.0 * GELU_1 * square)
+    return (values * gate).astype(BF16), slope
 
 
 def normalise(values):
@@ -624,7 +632,6 @@
         rows = slice(token * 256, token * 256 + 256)
         k_ref[rows] = mm(tokens, wk_ref[...]).astype(BF16)
         v_ref[rows] = mm(tokens, wv_ref[...]).astype(BF16)
-    kt_ref[...] = k_ref[...].T
     vt_ref[...] = v_ref[...].T
 
     def head_mask(head):
@@ -670,41 +677,44 @@
         edge.start()
         padded = pad_ref.at[layer]
         edge.fill_inner(padded)
-
+        if layer == 0:
+            kt_ref[...] = k_ref[...].T
+        else:
+
+            def slopes(part):
+                rows = pl.ds(aligned(part * 128, 128), 128)
+                dgelu_ref[0, rows] = gelu(dgelu_ref[0, rows])[1]
+
+            loop(0, 4, slopes)
         correlate(padded, taps_ref, layer, False, True, inner_ref, (1, 2))
         edge.fill_sides(padded)
         correlate(padded, taps_ref, layer, False, True, inner_ref, (0, 3))
         edge.fill_ends(padded)
         correlate(padded, taps_ref, layer, False, False, inner_ref, range(4))
 
-        def mix(row_pair):
-            top = aligned(row_pair * 2, 2)
+        def mix(part):
+            top = aligned(part * 8, 8)
             mixed = jnp.concatenate(
-                [inner_ref[0, pl.ds(top, 2)], inner_ref[1, pl.ds(top, 2)]], axis=-1
-            ).reshape(128, CH)
+                [inner_ref[0, pl.ds(top, 8)], inner_ref[1, pl.ds(top, 8)]], axis=-1
+            ).reshape(512, CH)
             xhat, scale = normalise(mixed)
-            rows = pl.ds(aligned(row_pair * 128, 128), 128)
+            rows = pl.ds(aligned(part * 512, 512), 512)
             xhat_ref[layer, rows] = xhat
-            rstd_ref[layer, rows] = jnp.broadcast_to(scale, (128, 128))
+            rstd_ref[layer, rows] = jnp.broadcast_to(scale, (512, 128))
             normed_low = xhat.astype(BF16)
             nrm_ref[layer, rows] = normed_low
             pre = mm(normed_low, we_ref[layer])
-            square = pre * pre
-            curve = jnp.tanh(pre * (GELU_0 + GELU_1 * square))
-            gate = 0.5 + 0.5 * curve
-            wide = (pre * gate).astype(BF16)
-            dgelu_ref[layer, rows] = gate + 0.5 * pre * (1.0 - curve * curve) * (
-                GELU_0 + 3.0 * GELU_1 * square
-            )
+            wide, slope = gelu(pre)
+            dgelu_ref[layer, rows] = pre if layer == 0 else slope
             wide_ref[layer, rows] = wide
-            before_mix = st_ref[layer, pl.ds(top, 2)].reshape(128, CH).astype(F32)
+            before_mix = st_ref[layer, pl.ds(top, 8)].reshape(512, CH).astype(F32)
             after = (before_mix + mm(wide, wr_ref[layer])).astype(BF16)
             if layer == 0:
-                st_ref[1, pl.ds(top, 2)] = after.reshape(2, COLS, CH)
+                st_ref[1, pl.ds(top, 8)] = after.reshape(8, COLS, CH)
             else:
                 analysis_ref[rows] = after
 
-        loop(0, 4, mix)
+        loop(0, 1, mix)
 
     kgrad_ref[...] = jnp.zeros_like(kgrad_ref)
     stores[0].start()
@@ -722,9 +732,9 @@
     for layer in (1, 0):
         sums = x_1 if layer == 1 else x_0
 
-        def unmix(row_pair):
-            top = aligned(row_pair * 2, 2)
-            rows = pl.ds(aligned(row_pair * 128, 128), 128)
+        def unmix(part):
+            top = aligned(part * 8, 8)
+            rows = pl.ds(aligned(part * 512, 512), 512)
             low = grad_ref[rows].astype(BF16)
             low_ref[rows] = low
             grad_pre = (mm_nt(low, wr_ref[layer]) * dgelu_ref[layer, rows]).astype(BF16)
@@ -737,9 +747,9 @@
                 - xhat * jnp.mean(grad_norm * xhat, axis=-1, keepdims=True)
             )
             grad_mixed = (centred * rstd_ref[layer, rows][:, :1]).astype(BF16)
-            gl_ref[layer, pl.ds(top, 2)] = grad_mixed.reshape(2, COLS, CH)
-
-        loop(0, 4, unmix)
+            gl_ref[layer, pl.ds(top, 8)] = grad_mixed.reshape(8, COLS, CH)
+
+        loop(0, 1, unmix)
         edge = halo(2 + layer, gl_ref.at[layer])
         edge.start()
         edge.fill_inner(pad_back)
@@ -828,7 +838,6 @@
     reduce_att.start_0()
     reduce_att.start_1()
     reduce_1.start_5()
-    reduce_0.start_4()
 
     end_hop(back_b, got_b, 2, NLON)
     for c in range(2):
@@ -838,6 +847,7 @@
     start_hop(along_lat, back_a, got_a, 3, NLAT)
     got_a[block(lat)] = back_a[block(lat)]
     reduce_att.start_2()
+    reduce_0.start_4()
     end_hop(back_a, got_a, 3, NLAT)
     grad_enc_ref[...] = mm_tn(chosen_ref[0], got_a[:, :512]) + mm_tn(chosen_ref[1], got_a[:, 512:])
     stores[1].start()

time: 128 us -> 122 us (0.953)
  Pallas kernels: 127 us -> 121 us
    pallas_call x1, Pallas kernels: 124 us -> 117 us  [fused(): pl.pallas_call(kernel, out_shape=results, in_specs=[pl.BlockSpec(memory_s...]
where the time goes in v3:
time: 122 us
  Pallas kernels  121 us (99%)
    pallas_call x1, Pallas kernels, fused(): pl.pallas_call(kernel, out_shape=results, in_specs=[pl.BlockSpec(memory_s...  117 us
    pallas_call x1, Pallas kernels, finished(): pl.pallas_call(finishing, out_shape=[jax.ShapeDtypeStruct((CELLS, CH), BF...  3.73 us

profile of v3, /device:TPU:1, one launch (start us, length us, event | category | flops | bytes accessed | tf_op | source)
XLA Modules:
  0.0 122.0 jit_solution(14905467257761140171)
XLA Ops:
  0.6 117.4 %assimilate.1 = (bf16[512,256]{1,0:T(8,128)(2,1)}, f32[96,512]{1,0:T(8,128)}, bf16[2304,128]{1,0:T(8,128)(2,1)}, bf16[2048,256]{1,0:T(8,128)(2,1)}, bf16[2048,256]{1,0:T(8,128)(2,1)}) custom-call(bf16[512,256]{1,0:T(8,128)(2,1)} %bitcast.6, bf16[96,2,256]{2,1,0:T(2,128)(2,1)} %enc_hbm.1, s32[2,12288]{1,0:T(2,128)} %bitcast.8, bf16[256,256]{1,0:T(8,128)(2,1)} %wq_hbm.1, ...), custom_call_target="tpu_custom_call" | custom-call | tf_op jit(solution)/shard_map/assimilate/pallas_call | solution.py:954
  118.1 3.7 %finish.1 = (bf16[512,256]{1,0:T(8,128)(2,1)}, f32[96,2,256]{2,1,0:T(2,128)}, f32[4,256,256]{2,1,0:T(8,128)}, f32[7,7,2,256]{3,2,1,0:T(2,128)}, f32[2,256,1024]{2,1,0:T(8,128)}, /*index=5*/f32[2,1024,256]{2,1,0:T(8,128)}) custom-call(bf16[512,256]{1,0:T(8,128)(2,1)} %get-tuple-element.17.analysis_hbm, f32[96,512]{1,0:T(8,128)} %get-tuple-element.18.grad_enc_hbm, ...), custom_call_target="tpu_custom_call" | custom-call | tf_op jit(solution)/shard_map/finish/pallas_call | solution.py:1059

commit v4 on v3

--- a/solution.py
+++ b/solution.py
@@ -816,11 +816,16 @@
             dq_t_ref[mine, :] = (mm(kt_ref[mine, :], grad_scores) * SCALE).astype(BF16)
 
     loop(0, 2, unattend)
+    reduce_0.start_2()
     reduce_1.start_4()
-    reduce_0.start_2()
     loop(2, 4, unattend)
     reduce_0.start_3()
 
+    put_attention(0, mm(dq_t_ref[...], normed_ref[...]).astype(BF16).T)
+    for index, grads in ((1, dk_t_ref), (2, dv_t_ref)):
+        sums = mm(grads[:, :256], recv_b[:, :CH]) + mm(grads[:, 256:], recv_b[:, CH:])
+        put_attention(index, sums.astype(BF16).T)
+    reduce_att.start_0()
     grad_keys = dk_t_ref[...].T
     grad_values = dv_t_ref[...].T
     for token in range(2):
@@ -828,16 +833,12 @@
         back_b[:, token * CH : token * CH + CH] = (
             mm_nt(grad_keys[rows], wk_ref[...]) + mm_nt(grad_values[rows], wv_ref[...])
         ).astype(BF16)
+    reduce_att.start_1()
     start_hop(along_lon, back_b, got_b, 2, NLON)
     got_b[block(lon)] = back_b[block(lon)]
-
-    put_attention(0, mm(dq_t_ref[...], normed_ref[...]).astype(BF16).T)
-    for index, grads in ((1, dk_t_ref), (2, dv_t_ref)):
-        sums = mm(grads[:, :256], recv_b[:, :CH]) + mm(grads[:, 256:], recv_b[:, CH:])
-        put_attention(index, sums.astype(BF16).T)
-    reduce_att.start_0()
-    reduce_att.start_1()
     reduce_1.start_5()
+    reduce_att.start_2()
+    reduce_0.start_4()
 
     end_hop(back_b, got_b, 2, NLON)
     for c in range(2):
@@ -846,14 +847,12 @@
         ).astype(BF16)
     start_hop(along_lat, back_a, got_a, 3, NLAT)
     got_a[block(lat)] = back_a[block(lat)]
-    reduce_att.start_2()
-    reduce_0.start_4()
+    reduce_1.finish()
+    stores[3].start()
+    reduce_att.start_3()
     end_hop(back_a, got_a, 3, NLAT)
     grad_enc_ref[...] = mm_tn(chosen_ref[0], got_a[:, :512]) + mm_tn(chosen_ref[1], got_a[:, 512:])
     stores[1].start()
-    reduce_1.finish()
-    stores[3].start()
-    reduce_att.start_3()
     reduce_0.start_5()
     reduce_att.start_5()
     reduce_0.finish()

time: 122 us -> 118 us (0.967)
  Pallas kernels: 121 us -> 117 us
    pallas_call x1, Pallas kernels: 117 us -> 113 us  [fused(): pl.pallas_call(kernel, out_shape=results, in_specs=[pl.BlockSpec(memory_s...]
where the time goes in v4:
time: 118 us
  Pallas kernels  117 us (99%)
    pallas_call x1, Pallas kernels, fused(): pl.pallas_call(kernel, out_shape=results, in_specs=[pl.BlockSpec(memory_s...  113 us
    pallas_call x1, Pallas kernels, finished(): pl.pallas_call(finishing, out_shape=[jax.ShapeDtypeStruct((CELLS, CH), BF...  3.73 us

profile of v4, /device:TPU:1, one launch (start us, length us, event | category | flops | bytes accessed | tf_op | source)
XLA Modules:
  0.0 117.6 jit_solution(12946446329622756526)
XLA Ops:
  0.6 113.0 %assimilate.1 = (bf16[512,256]{1,0:T(8,128)(2,1)}, f32[96,512]{1,0:T(8,128)}, bf16[2304,128]{1,0:T(8,128)(2,1)}, bf16[2048,256]{1,0:T(8,128)(2,1)}, bf16[2048,256]{1,0:T(8,128)(2,1)}) custom-call(bf16[512,256]{1,0:T(8,128)(2,1)} %bitcast.6, bf16[96,2,256]{2,1,0:T(2,128)(2,1)} %enc_hbm.1, s32[2,12288]{1,0:T(2,128)} %bitcast.8, bf16[256,256]{1,0:T(8,128)(2,1)} %wq_hbm.1, ...), custom_call_target="tpu_custom_call" | custom-call | tf_op jit(solution)/shard_map/assimilate/pallas_call | solution.py:953
  113.7 3.7 %finish.1 = (bf16[512,256]{1,0:T(8,128)(2,1)}, f32[96,2,256]{2,1,0:T(2,128)}, f32[4,256,256]{2,1,0:T(8,128)}, f32[7,7,2,256]{3,2,1,0:T(2,128)}, f32[2,256,1024]{2,1,0:T(8,128)}, /*index=5*/f32[2,1024,256]{2,1,0:T(8,128)}) custom-call(bf16[512,256]{1,0:T(8,128)(2,1)} %get-tuple-element.17.analysis_hbm, f32[96,512]{1,0:T(8,128)} %get-tuple-element.18.grad_enc_hbm, ...), custom_call_target="tpu_custom_call" | custom-call | tf_op jit(solution)/shard_map/finish/pallas_call | solution.py:1058
